TPU v7x, 32 devices: a whole 2x2x4 slice. The times are simulated.
32 devices in a mesh: lev: 2 (over y), lat: 16 (over z, x, core).
Axes of the slice: x: 2, y: 2, z: 4, core: 2. Of those that a mesh axis runs over, the one named last changes fastest.
Arguments:
- tl_pert: float32 [8, 8, 32, 1440], P(None, 'lev', 'lat'), may hold values from -6 to 6
- adj_in: float32 [8, 8, 32, 1440], P(None, 'lev', 'lat'), may hold values from -6 to 6
- zonal_wind: float32 [8, 32, 1440], P('lev', 'lat'), may hold values from -3 to 3
- merid_wind: float32 [8, 32, 1440], P('lev', 'lat'), may hold values from -3 to 3
- vert_wind: float32 [8, 32, 1440], P('lev', 'lat'), may hold values from -3 to 3
- cutoffs: int32 [32], P('lat'), may hold values from 540 to 720
- remap: float32 [8, 8, 8], replicated, may hold values from -1.5 to 1.5
- phys_op: float32 [8, 8, 8], replicated, may hold values from -1 to 1
- phys_state: float32 [8, 32, 1440], P(None, 'lat', 'lev'), may hold values from 0.6 to 1.4
- column_cost: int32 [32, 2], P('lat', 'lev'), may hold values from 1 to 8, as said below
Outputs:
- tl_out: float32 [8, 8, 32, 1440], P(None, 'lev', 'lat')
- adj_out: float32 [8, 8, 32, 1440], P(None, 'lev', 'lat')
Inputs may be any that keep to these rules, and one draw needn't show every extreme that they name: `column_cost`: the value 8 occurs in every draw.
All inputs are finite; a program needn't handle non-finite values.
Results may differ from a plain program's by a relative error of at most 0.0003.
Values sent between devices are 32-bit elements; how exact they have to be, the bound alone decides.
A program may use at most 64 MiB of HBM per device.

v0:
```python
import functools
import math

import jax
import jax.numpy as jnp
import ml_dtypes
import numpy as np
from jax import lax
from jax.experimental import pallas as pl
from jax.experimental.pallas import tpu as pltpu
from jax.sharding import PartitionSpec as P

SUBS = 8


HIGHEST = lax.Precision.HIGHEST


def with_halo(cells, sides, width):
    for axis, dim in sides:
        count = lax.axis_size(axis)
        ends = count - 1
        head = lax.slice_in_dim(cells, 0, width, axis=dim)
        tail = lax.slice_in_dim(cells, cells.shape[dim] - width, cells.shape[dim], axis=dim)
        cells = jnp.concatenate(
            [
                lax.ppermute(tail, axis, [(i, (i + 1) % count) for i in range(ends)]),
                cells,
                lax.ppermute(head, axis, [((i + 1) % count, i) for i in range(ends)]),
            ],
            axis=dim,
        )
    return cells


def fourier_basis(length):
    sample = jnp.arange(length, dtype=jnp.int32)[:, None]
    column = jnp.arange(length, dtype=jnp.int32)[None, :]
    nyquist = length // 2
    wavenumber = jnp.where(column <= nyquist, column, column - nyquist)
    angles = (sample * wavenumber % length).astype(jnp.float32) * (2.0 * math.pi / length)
    weights = jnp.where(
        (wavenumber == 0) | (wavenumber == nyquist),
        1.0 / math.sqrt(length),
        math.sqrt(2.0 / length),
    )
    basis_table = jnp.where(column <= nyquist, jnp.cos(angles), jnp.sin(angles)) * weights
    return (basis_table, wavenumber[0])


def upper_modes(length):
    basis_table, wavenumber = fourier_basis(length)
    nyquist = length // 2
    lowest = 3 * length // 8 + 1
    cosine_part = basis_table[:, lowest : nyquist + 1]
    sine_part = basis_table[:, nyquist + lowest :]
    modes = jnp.concatenate([cosine_part, sine_part], axis=1)
    mode_numbers = jnp.concatenate(
        [wavenumber[lowest : nyquist + 1], wavenumber[nyquist + lowest :]]
    )
    return (modes, mode_numbers)


def polar_filter(grid_field, drop_mask, modes):
    coeffs = jnp.einsum("fkix,xc->fkic", grid_field, modes, precision=HIGHEST)
    return grid_field - jnp.einsum("fkic,xc->fkix", coeffs * drop_mask, modes, precision=HIGHEST)


def tangent_advect(grid_field, zonal_wind, merid_wind, vert_wind):
    padded = with_halo(grid_field, (("lev", 1), ("lat", 2)), 1)
    lat_diff = padded[:, 1:-1, 2:] - padded[:, 1:-1, :-2]
    lev_diff = padded[:, 2:, 1:-1] - padded[:, :-2, 1:-1]
    lon_diff = jnp.roll(grid_field, -1, axis=3) - jnp.roll(grid_field, 1, axis=3)
    return grid_field - 0.5 * (zonal_wind * lon_diff + merid_wind * lat_diff + vert_wind * lev_diff)


def adjoint_advect(grid_field, zonal_wind, merid_wind, vert_wind):
    merid_padded = with_halo(merid_wind * grid_field, (("lat", 2),), 1)
    vert_padded = with_halo(vert_wind * grid_field, (("lev", 1),), 1)
    zonal_part = zonal_wind * grid_field
    lon_term = jnp.roll(zonal_part, -1, axis=3) - jnp.roll(zonal_part, 1, axis=3)
    lat_term = merid_padded[:, :, 2:] - merid_padded[:, :, :-2]
    lev_term = vert_padded[:, 2:] - vert_padded[:, :-2]
    return grid_field + 0.5 * (lon_term + lat_term + lev_term)


def to_columns(stacked):
    return lax.all_to_all(stacked, "lev", split_axis=4, concat_axis=2, tiled=True)


def to_bands(stacked):
    return lax.all_to_all(stacked, "lev", split_axis=2, concat_axis=4, tiled=True)


def column_physics(operators, state_rows, fields_all, row_counts):
    unit_rows = jnp.ones_like(state_rows)
    before = jnp.stack([state_rows, unit_rows])[:, None]
    after = jnp.stack([unit_rows, state_rows])[:, None]
    counts_view = row_counts[None, None, None, :, None]
    current = fields_all
    for sub_step in range(SUBS):
        advanced = after * jnp.einsum(
            "sfkl,sflix->sfkix", operators, before * current, precision=HIGHEST
        )
        current = jnp.where(sub_step < counts_view, advanced, current)
    return current


def local(
    tl_pert,
    adj_in,
    zonal_wind,
    merid_wind,
    vert_wind,
    cutoffs,
    remap,
    phys_op,
    phys_state,
    column_cost,
):
    modes, mode_numbers = upper_modes(tl_pert.shape[3])
    drop_mask = (mode_numbers[None, :] > cutoffs[:, None]).astype(jnp.float32)
    operators = jnp.stack([phys_op, jnp.swapaxes(phys_op, 1, 2)])
    row_counts = column_cost[:, 0]
    adj_columns = to_columns(adj_in[None])
    tl_advected = tangent_advect(tl_pert, zonal_wind, merid_wind, vert_wind)
    tl_filtered = polar_filter(tl_advected, drop_mask, modes)
    tl_columns = to_columns(tl_filtered[None])
    tl_remapped = jnp.einsum("fkl,sflix->sfkix", remap, tl_columns, precision=HIGHEST)
    fields_all = jnp.concatenate([tl_remapped, adj_columns], axis=0)
    physics_done = column_physics(operators, phys_state, fields_all, row_counts)
    tl_finished = physics_done[0:1]
    adj_remapped = jnp.einsum("flk,sflix->sfkix", remap, physics_done[1:2], precision=HIGHEST)
    tl_result = to_bands(tl_finished)[0]
    adj_bands = to_bands(adj_remapped)[0]
    adj_filtered = polar_filter(adj_bands, drop_mask, modes)
    adj_result = adjoint_advect(adj_filtered, zonal_wind, merid_wind, vert_wind)
    return (tl_result, adj_result)

BF16 = jnp.bfloat16
F32 = jnp.float32
LANES = 128
MODES = 256
MESH_IDS = pl.DeviceIdType.MESH


def mode_tables(length, half, padded):
    nyquist = length // 2
    lowest = 3 * length // 8 + 1
    forward = np.zeros((2, 2, padded, MODES), ml_dtypes.bfloat16)
    backward = np.zeros((2, 2, MODES, padded), ml_dtypes.bfloat16)
    numbers = np.zeros((2, MODES), np.int32)
    sample = np.arange(half)
    for parity in range(2):
        cosines = [m for m in range(lowest, nyquist + 1) if m % 2 == parity]
        sines = [m for m in range(lowest, nyquist) if m % 2 == parity]
        waves = np.array(cosines + sines)
        count = len(waves)
        angles = 2.0 * np.pi / length * ((sample[:, None] * waves[None, :]) % length)
        is_cosine = (np.arange(count) < len(cosines))[None, :]
        weight = np.where(waves == nyquist, length**-0.5, (2.0 / length) ** 0.5)
        table = np.where(is_cosine, np.cos(angles), np.sin(angles)) * weight[None, :]
        high = table.astype(ml_dtypes.bfloat16)
        low = (table - high.astype(np.float64)).astype(ml_dtypes.bfloat16)
        for part, piece in enumerate((high, low)):
            forward[parity, part, :half, :count] = piece
            backward[parity, part, :count, :half] = piece.T
        numbers[parity, :count] = waves
    return forward, backward, numbers


def split_dot(rows, high, low):
    count = rows.shape[0]
    top = rows.astype(BF16)
    rest = (rows - top.astype(F32)).astype(BF16)
    both = jnp.dot(jnp.concatenate([top, rest], axis=0), high, preferred_element_type=F32)
    cross = jnp.dot(top, low, preferred_element_type=F32)
    return both[:count] + both[count:] + cross


def filter_in_place(buf, levels, mask, fwd, bwd):
    width = buf.shape[-1]
    rows = levels * 16
    first = buf[0].reshape(rows, width)
    second = buf[1].reshape(rows, width)
    dropped = []
    for parity, folded in enumerate((first + second, first - second)):
        coeffs = split_dot(folded, fwd[parity, 0], fwd[parity, 1])
        kept = coeffs.reshape(levels, 2, 8, MODES) * mask[parity][None]
        dropped.append(split_dot(kept.reshape(rows, MODES), bwd[parity, 0], bwd[parity, 1]))
    even, odd = dropped
    buf[0] = (first - (even + odd)).reshape(levels, 2, 8, width)
    buf[1] = (second - (even - odd)).reshape(levels, 2, 8, width)


def step_kernel(
    half,
    bands,
    tl,
    adj,
    winds,
    ops,
    counts,
    mask,
    fwd_hbm,
    bwd_hbm,
    out_tl,
    out_adj,
    fwd,
    bwd,
    qx,
    wext,
    acols,
    tbuf,
    tcols,
    aback,
    tback,
    abuf,
    mx,
    vx,
    mats,
    send_sem,
    recv_sem,
    load_sem,
):
    width = tl.shape[-1]
    tiles = width // LANES
    lev = lax.axis_index("lev")
    lat = lax.axis_index("lat")
    other = 1 - lev
    has_up = lat < bands - 1
    has_down = lat > 0

    loads = [
        pltpu.make_async_copy(fwd_hbm, fwd, load_sem.at[0]),
        pltpu.make_async_copy(bwd_hbm, bwd, load_sem.at[1]),
    ]

    barrier = pltpu.get_barrier_semaphore()
    pl.semaphore_signal(barrier, inc=1, device_id=(other, lat), device_id_type=MESH_IDS)

    @pl.when(has_up)
    def _():
        pl.semaphore_signal(barrier, inc=1, device_id=(lev, lat + 1), device_id_type=MESH_IDS)

    @pl.when(has_down)
    def _():
        pl.semaphore_signal(barrier, inc=1, device_id=(lev, lat - 1), device_id_type=MESH_IDS)

    inner = jnp.logical_and(has_up, has_down)

    @pl.when(inner)
    def _():
        pl.semaphore_wait(barrier, 3)

    @pl.when(jnp.logical_not(inner))
    def _():
        pl.semaphore_wait(barrier, 2)

    def remote(number, src, dst, to_lev, to_lat):
        return pltpu.make_async_remote_copy(
            src_ref=src,
            dst_ref=dst,
            send_sem=send_sem.at[number],
            recv_sem=recv_sem.at[number],
            device_id=(to_lev, to_lat),
            device_id_type=MESH_IDS,
        )

    edge = 3 * other
    lev_halo = remote(0, tl.at[:, edge], qx.at[:, 5 * lev, pl.ds(1, 2)], other, lat)
    lat_up = remote(1, tl.at[:, :, 1], qx.at[:, pl.ds(1, 4), 0], lev, lat + 1)
    lat_down = remote(2, tl.at[:, :, 0], qx.at[:, pl.ds(1, 4), 3], lev, lat - 1)
    wind_halo = remote(3, winds.at[edge, pl.ds(8, 8)], wext, other, lat)
    mine = pl.ds(4 * lev, 4)
    theirs = pl.ds(4 * other, 4)
    adj_out_cols = [
        remote(4 + i, adj.at[other, :, i], acols.at[mine, i], other, lat) for i in range(2)
    ]
    adj_in_bands = [
        remote(6 + i, aback.at[pl.ds(3 * other, 5), i], abuf.at[lev, :, i], other, lat)
        for i in range(2)
    ]
    tl_out_cols = [
        remote(8 + i, tbuf.at[other, :, i], tcols.at[mine, i], other, lat) for i in range(2)
    ]
    tl_in_bands = [
        remote(10 + i, tback.at[theirs, i], out_tl.at[lev, :, i], other, lat) for i in range(2)
    ]
    merid_up = remote(12, mx.at[:, :, 2], mx.at[:, :, 0], lev, lat + 1)
    merid_down = remote(13, mx.at[:, :, 1], mx.at[:, :, 3], lev, lat - 1)

    lev_halo.start()

    @pl.when(has_up)
    def _():
        lat_up.start()

    @pl.when(has_down)
    def _():
        lat_down.start()

    wind_halo.start()
    for copy in adj_out_cols:
        copy.start()
    for load in loads:
        load.start()

    zeros = jnp.zeros((8, width), F32)

    @pl.when(jnp.logical_not(has_down))
    def _():
        for h in range(2):
            for k in range(4):
                qx[h, 1 + k, 0] = zeros
                mx[h, k, 0] = zeros

    @pl.when(jnp.logical_not(has_up))
    def _():
        for h in range(2):
            for k in range(4):
                qx[h, 1 + k, 3] = zeros
                mx[h, k, 3] = zeros

    for h in range(2):
        for i in range(2):
            qx[h, 5 * lev, 1 + i] = zeros
            vx[h, 5 * lev, i] = zeros
    qx[:, 1:5, 1:3] = tl[...]
    acols[mine] = adj[lev]

    table = ops[...]
    for entry in range(128):
        mats[entry] = jnp.broadcast_to(table[:, entry : entry + 1], (8, LANES))

    lane = lax.broadcasted_iota(jnp.int32, (8, width), 1)

    def wind(ref_row):
        return jnp.broadcast_to(ref_row, (8, width))

    def lon_diff(z, across):
        after = jnp.where(lane == half - 1, across[:, 0:1], pltpu.roll(z, width - 1, 1))
        before = jnp.where(lane == 0, across[:, half - 1 : half], pltpu.roll(z, 1, 1))
        return after - before

    lev_halo.wait_recv()

    @pl.when(has_down)
    def _():
        lat_up.wait_recv()

    @pl.when(has_up)
    def _():
        lat_down.wait_recv()

    def advect(k, carry):
        for h in range(2):
            for i in range(2):
                row = 2 * h + i
                q = qx[h, k + 1, i + 1]
                zonal = wind(winds[k, row : row + 1]) * lon_diff(q, qx[1 - h, k + 1, i + 1])
                merid = wind(winds[k, 4 + row : 5 + row]) * (
                    qx[h, k + 1, i + 2] - qx[h, k + 1, i]
                )
                vert = wind(winds[k, 8 + row : 9 + row]) * (
                    qx[h, k + 2, i + 1] - qx[h, k, i + 1]
                )
                tbuf[h, k, i] = q - 0.5 * (zonal + merid + vert)
        return carry

    lax.fori_loop(0, 4, advect, 0)
    for load in loads:
        load.wait()
    filter_in_place(tbuf, 4, mask, fwd, bwd)
    for copy in tl_out_cols:
        copy.start()
    tcols[mine] = tbuf[lev]

    def product(base, transposed, vec):
        result = []
        for k in range(8):
            terms = [
                mats[base + (8 * l + k if transposed else 8 * k + l)] * vec[l] for l in range(8)
            ]
            while len(terms) > 1:
                terms = [a + b for a, b in zip(terms[::2], terms[1::2])]
            result.append(terms[0])
        return result

    def physics(src, dst, i, adjoint):
        steps = counts[i]

        def tile(t, carry):
            cols = pl.ds(pl.multiple_of(t * LANES, LANES), LANES)
            state = [
                jnp.broadcast_to(
                    winds[l // 2, 12 + 2 * (l % 2) + i : 13 + 2 * (l % 2) + i, cols], (8, LANES)
                )
                for l in range(8)
            ]
            vec = [src[l, i, :, cols] for l in range(8)]
            if not adjoint:
                vec = product(64, False, vec)

            def sub_step(s, vec):
                if adjoint:
                    new = [d * v for d, v in zip(state, product(0, True, vec))]
                else:
                    new = product(0, False, [d * v for d, v in zip(state, vec)])
                active = s < steps
                return [jnp.where(active, n, v) for n, v in zip(new, vec)]

            vec = lax.fori_loop(0, SUBS, sub_step, vec)
            if adjoint:
                vec = product(64, True, vec)
            for k in range(8):
                dst[k, i, :, cols] = vec[k]
            return carry

        lax.fori_loop(0, tiles, tile, 0)

    for i in range(2):
        adj_out_cols[i].wait_recv()
        physics(acols, aback, i, True)
        adj_in_bands[i].start()
    abuf[lev] = aback[pl.ds(3 * lev, 5)]

    for i in range(2):
        tl_out_cols[i].wait_recv()
        physics(tcols, tback, i, False)
        tl_in_bands[i].start()
    out_tl[lev] = tback[mine]

    wind_halo.wait_recv()
    for i in range(2):
        adj_in_bands[i].wait_recv()
    filter_in_place(abuf, 5, mask, fwd, bwd)

    def merid_parts(k, carry):
        for h in range(2):
            for i in range(2):
                row = 2 * h + i
                mx[h, k, i + 1] = wind(winds[k, 4 + row : 5 + row]) * abuf[h, k + lev, i]
        return carry

    lax.fori_loop(0, 4, merid_parts, 0)

    @pl.when(has_up)
    def _():
        merid_up.start()

    @pl.when(has_down)
    def _():
        merid_down.start()

    def vert_parts(k, carry):
        for h in range(2):
            for i in range(2):
                row = 2 * h + i
                vx[h, k + 1, i] = wind(winds[k, 8 + row : 9 + row]) * abuf[h, k + lev, i]
        return carry

    lax.fori_loop(0, 4, vert_parts, 0)
    for h in range(2):
        for i in range(2):
            row = 2 * h + i
            vx[h, 5 * other, i] = wind(wext[row : row + 1]) * abuf[h, 4 * other, i]

    def zonal_parts(k, carry):
        for i in range(2):
            p = [abuf[h, k + lev, i] for h in range(2)]
            z = [wind(winds[k, 2 * h + i : 2 * h + i + 1]) * p[h] for h in range(2)]
            for h in range(2):
                total = lon_diff(z[h], z[1 - h]) + (vx[h, k + 2, i] - vx[h, k, i])
                out_adj[h, k, i] = p[h] + 0.5 * total
        return carry

    lax.fori_loop(0, 4, zonal_parts, 0)

    @pl.when(has_down)
    def _():
        merid_up.wait_recv()

    @pl.when(has_up)
    def _():
        merid_down.wait_recv()

    def add_merid(k, carry):
        for h in range(2):
            for i in range(2):
                out_adj[h, k, i] = out_adj[h, k, i] + 0.5 * (mx[h, k, i + 2] - mx[h, k, i])
        return carry

    lax.fori_loop(0, 4, add_merid, 0)

    for copy in tl_in_bands:
        copy.wait_recv()
    for copy in [lev_halo, wind_halo] + adj_out_cols + adj_in_bands + tl_out_cols + tl_in_bands:
        copy.wait_send()

    @pl.when(has_up)
    def _():
        lat_up.wait_send()
        merid_up.wait_send()

    @pl.when(has_down)
    def _():
        lat_down.wait_send()
        merid_down.wait_send()


def one_kernel(
    tl_pert,
    adj_in,
    zonal_wind,
    merid_wind,
    vert_wind,
    cutoffs,
    remap,
    phys_op,
    phys_state,
    column_cost,
):
    length = tl_pert.shape[3]
    half = length // 2
    padded = -(-half // LANES) * LANES
    spare = padded - half
    bands = lax.axis_size("lat")
    forward, backward, numbers = mode_tables(length, half, padded)

    def to_kernel(field):
        halves = field.reshape(8, 4, 2, 2, half).transpose(3, 1, 2, 0, 4)
        return jnp.pad(halves, ((0, 0),) * 4 + ((0, spare),))

    def from_kernel(field):
        return field[..., :half].transpose(3, 1, 2, 0, 4).reshape(8, 4, 2, length)

    def wind_rows(field):
        return field.reshape(4, 2, 2, half).transpose(0, 2, 1, 3).reshape(4, 4, half)

    winds = jnp.concatenate(
        [
            wind_rows(zonal_wind),
            wind_rows(merid_wind),
            wind_rows(vert_wind),
            phys_state.reshape(4, 4, half),
        ],
        axis=1,
    )
    winds = jnp.pad(winds, ((0, 0), (0, 0), (0, spare)))
    ops = jnp.concatenate([phys_op.reshape(8, 64), remap.reshape(8, 64)], axis=1)
    counts = jnp.broadcast_to(column_cost[:, :, None], (2, 8, LANES))
    drop = (jnp.asarray(numbers)[:, None, None, :] > cutoffs[None, :, None, None]).astype(F32)
    mask = jnp.broadcast_to(drop, (2, 2, 8, MODES))

    vmem = pl.BlockSpec(memory_space=pltpu.VMEM)
    hbm = pl.BlockSpec(memory_space=pl.ANY)
    band_shape = (2, 4, 2, 8, padded)
    column_shape = (8, 2, 8, padded)
    outs = pl.pallas_call(
        functools.partial(step_kernel, half, bands),
        out_shape=[jax.ShapeDtypeStruct(band_shape, F32)] * 2,
        in_specs=[vmem] * 6 + [hbm] * 2,
        out_specs=[vmem] * 2,
        scratch_shapes=[
            pltpu.VMEM(forward.shape, BF16),
            pltpu.VMEM(backward.shape, BF16),
            pltpu.VMEM((2, 6, 4, 8, padded), F32),
            pltpu.VMEM((8, padded), F32),
            pltpu.VMEM(column_shape, F32),
            pltpu.VMEM(band_shape, F32),
            pltpu.VMEM(column_shape, F32),
            pltpu.VMEM(column_shape, F32),
            pltpu.VMEM(column_shape, F32),
            pltpu.VMEM((2, 5, 2, 8, padded), F32),
            pltpu.VMEM((2, 4, 4, 8, padded), F32),
            pltpu.VMEM((2, 6, 2, 8, padded), F32),
            pltpu.VMEM((128, 8, LANES), F32),
            pltpu.SemaphoreType.DMA((14,)),
            pltpu.SemaphoreType.DMA((14,)),
            pltpu.SemaphoreType.DMA((2,)),
        ],
        compiler_params=pltpu.CompilerParams(
            collective_id=0, has_side_effects=True, vmem_limit_bytes=40 * 1024 * 1024
        ),
        cost_estimate=pl.CostEstimate(
            flops=10**9, bytes_accessed=8 * 10**6, transcendentals=0
        ),
    )(
        to_kernel(tl_pert),
        to_kernel(adj_in),
        winds,
        ops,
        counts,
        mask,
        jnp.asarray(forward),
        jnp.asarray(backward),
    )
    return from_kernel(outs[0]), from_kernel(outs[1])


def fits_kernel(mesh):
    return mesh.shape["lev"] == 2 and mesh.shape["lat"] > 1


def solution(mesh):
    placed = (
        P(None, "lev", "lat", None),
        P(None, "lev", "lat", None),
        P("lev", "lat", None),
        P("lev", "lat", None),
        P("lev", "lat", None),
        P("lat"),
        P(),
        P(),
        P(None, "lat", "lev"),
        P("lat", "lev"),
    )
    return jax.shard_map(
        one_kernel if fits_kernel(mesh) else local,
        mesh=mesh,
        in_specs=placed,
        out_specs=(P(None, "lev", "lat", None), P(None, "lev", "lat", None)),
        check_vma=False,
    )
```

profile of v0, /device:TPU:1, one launch (start us, length us, event | category | flops | bytes accessed | tf_op | source)
XLA Modules:
  0.0 47.3 jit_solution(6324151042415807303)
XLA Ops:
  0.6 0.0 copy-start.4
  0.6 0.8 %compare_convert_fusion = f32[2,2,256]{2,1,0:T(2,128)S(1)} fusion(s32[2,256]{1,0:T(2,128)} %constant.9.clone, s32[2]{0:T(128)} %param.18), kind=kLoop, calls=%fused_computation.11 | loop fusion | flops 2048 | bytes 6152 | tf_op jit(solution)/shard_map/convert_element_type | solution.py:553
  1.4 0.8 %reshape.64 = f32[8,64]{1,0:T(8,128)S(1)} reshape(f32[8,8,8]{2,1,0:T(8,128)} %param.19) | data formatting | bytes 4096 | tf_op jit(solution)/shard_map/reshape | solution.py:551
  2.3 0.8 %reshape.63 = f32[8,64]{1,0:T(8,128)S(1)} reshape(f32[8,8,8]{2,1,0:T(8,128)} %param.20) | data formatting | bytes 4096 | tf_op jit(solution)/shard_map/reshape | solution.py:551
  3.1 0.1 pad_maximum_fusion.ops
  3.2 0.7 %broadcast_in_dim.7.counts = s32[2,8,128]{2,1,0:T(8,128)S(1)} broadcast(s32[2]{0:T(128)} %bitcast.25), dimensions={0} | broadcast | bytes 8200 | tf_op jit(solution)/shard_map/broadcast_in_dim | solution.py:552
  3.9 0.6 %broadcast_in_dim.8.mask = f32[2,2,8,256]{3,2,1,0:T(8,128)} broadcast(f32[2,2,256]{2,1,0:T(2,128)S(1)} %compare_convert_fusion), dimensions={0,1,3} | broadcast | bytes 36864 | tf_op jit(solution)/shard_map/broadcast_in_dim | solution.py:554
  4.5 0.9 %reshape.56 = f32[4,2,2,720]{3,2,1,0:T(2,128)S(1)} reshape(f32[4,2,1440]{2,1,0:T(2,128)} %param.15) | data formatting | bytes 92160 | tf_op jit(solution)/shard_map/reshape | solution.py:539
  5.5 0.9 %reshape.58 = f32[4,2,2,720]{3,2,1,0:T(2,128)S(1)} reshape(f32[4,2,1440]{2,1,0:T(2,128)} %param.16) | data formatting | bytes 92160 | tf_op jit(solution)/shard_map/reshape | solution.py:539
  6.6 0.9 %reshape.60 = f32[4,2,2,720]{3,2,1,0:T(2,128)S(1)} reshape(f32[4,2,1440]{2,1,0:T(2,128)} %param.17) | data formatting | bytes 92160 | tf_op jit(solution)/shard_map/reshape | solution.py:539
  7.6 0.8 %reshape.62 = f32[4,4,720]{2,1,0:T(4,128)S(1)} reshape(f32[8,2,720]{2,1,0:T(2,128)} %param.21) | data formatting | bytes 92160 | tf_op jit(solution)/shard_map/reshape | solution.py:546
  8.4 0.7 %select_maximum_fusion.winds = f32[4,16,768]{2,1,0:T(8,128)} fusion(f32[4,4,720]{2,1,0:T(4,128)S(1)} %reshape.62, f32[4,4,720]{2,1,0:T(4,128)S(1)} %reshape.61, f32[4,4,720]{2,1,0:T(4,128)S(1)} %reshape.59, f32[4,4,720]{2,1,0:T(4,128)S(1)} %reshape.57), kind=kLoop, calls=%fused_computation.4 | loop fusion | flops 393216 | bytes 380928 | tf_op jit(solution)/shard_map/concatenate | solution.py:541
  9.1 0.0 copy-done.4
  9.2 0.6 %reshape.67 = f32[8,4,2,2,720]{4,3,2,1,0:T(2,128)S(1)} reshape(f32[8,4,2,1440]{3,2,1,0:T(2,128)S(1)} %copy-done.4) | data formatting | bytes 737280 | tf_op jit(solution)/shard_map/reshape | solution.py:532
  9.7 0.2 copy.43
  9.9 0.0 copy-start
  10.0 0.0 copy-start.1
  10.0 2.4 %reshape.68 = f32[8,4,2,2,720]{4,3,2,1,0:T(2,128)} reshape(f32[8,4,2,1440]{3,2,1,0:T(2,128)} %param.14) | data formatting | bytes 737280 | tf_op jit(solution)/shard_map/reshape | solution.py:532
  12.5 1.2 %copy.42 = f32[8,4,2,2,720]{4,0,2,1,3:T(8,128)S(1)} copy(f32[8,4,2,2,720]{4,3,2,1,0:T(2,128)} %reshape.68) | data formatting | bytes 737280 | tf_op jit(solution)/shard_map/reshape | solution.py:532
  13.7 0.0 copy-done
  13.7 0.0 copy-done.1
  13.7 0.0 copy-start.2
  13.8 0.9 %copy-done.2 = f32[4,16,768]{2,1,0:T(8,128)S(1)} copy-done((f32[4,16,768]{2,1,0:T(8,128)S(1)}, f32[4,16,768]{2,1,0:T(8,128)}, u32[]{:S(2)}) %copy-start.2) | copy-done | bytes 196632
  14.7 0.0 copy-start.3
  14.7 0.8 %copy-done.3 = f32[2,2,8,256]{3,2,1,0:T(8,128)S(1)} copy-done((f32[2,2,8,256]{3,2,1,0:T(8,128)S(1)}, f32[2,2,8,256]{3,2,1,0:T(8,128)}, u32[]{:S(2)}) %copy-start.3) | copy-done | bytes 32792
  15.4 28.6 %shard_map.140 = (f32[2,4,2,8,768]{4,3,2,1,0:T(8,128)S(1)}, f32[2,4,2,8,768]{4,3,2,1,0:T(8,128)S(1)}) custom-call(f32[2,4,2,8,768]{4,3,2,1,0:T(8,128)S(1)} %pad.11.tl, f32[2,4,2,8,768]{4,3,2,1,0:T(8,128)S(1)} %pad.12.adj, f32[4,16,768]{2,1,0:T(8,128)S(1)} %copy-done.2, f32[8,128]{1,0:T(8,128)S(1)} %pad_maximum_fusion.ops, ...), custom_call_target="tpu_custom_call" | custom-call | flops 1000000000 | bytes 8000000 | tf_op jit(solution)/shard_map/pallas_call | solution.py:560
  44.0 0.1 slice_bitcast_fusion
  44.1 0.3 copy.34
  44.4 1.3 %reshape.70 = f32[8,4,2,1440]{3,2,1,0:T(2,128)} reshape(f32[8,4,2,2,720]{4,3,2,1,0:T(2,128)S(1)} %copy.34) | data formatting | bytes 737280
  45.7 0.3 copy.33
  46.0 1.3 %reshape.69 = f32[8,4,2,1440]{3,2,1,0:T(2,128)} reshape(f32[8,4,2,2,720]{4,3,2,1,0:T(2,128)S(1)} %copy.33) | data formatting | bytes 737280
  (8 shorter events, 0.3 us)
Async XLA Ops:
  0.6 8.5 %copy-start.4 = (f32[8,4,2,1440]{3,2,1,0:T(2,128)S(1)}, f32[8,4,2,1440]{3,2,1,0:T(2,128)}, u32[]{:S(2)}) copy-start(f32[8,4,2,1440]{3,2,1,0:T(2,128)} %param.13) | copy-start | bytes 1105924
  9.9 3.8 %copy-start = (bf16[2,2,256,768]{3,2,1,0:T(8,128)(2,1)S(1)}, bf16[2,2,256,768]{3,2,1,0:T(8,128)(2,1)}, u32[]{:S(2)}) copy-start(bf16[2,2,256,768]{3,2,1,0:T(8,128)(2,1)} %constant.11.clone.bwd_hbm) | copy-start | bytes 4718596
  10.0 3.8 %copy-start.1 = (bf16[2,2,768,256]{3,2,1,0:T(8,128)(2,1)S(1)}, bf16[2,2,768,256]{3,2,1,0:T(8,128)(2,1)}, u32[]{:S(2)}) copy-start(bf16[2,2,768,256]{3,2,1,0:T(8,128)(2,1)} %constant.10.clone.fwd_hbm) | copy-start | bytes 4718596
  13.7 0.9 %copy-start.2 = (f32[4,16,768]{2,1,0:T(8,128)S(1)}, f32[4,16,768]{2,1,0:T(8,128)}, u32[]{:S(2)}) copy-start(f32[4,16,768]{2,1,0:T(8,128)} %select_maximum_fusion.winds) | copy-start | bytes 589828
  14.7 0.8 %copy-start.3 = (f32[2,2,8,256]{3,2,1,0:T(8,128)S(1)}, f32[2,2,8,256]{3,2,1,0:T(8,128)}, u32[]{:S(2)}) copy-start(f32[2,2,8,256]{3,2,1,0:T(8,128)} %broadcast_in_dim.8.mask) | copy-start | bytes 98308
where the time goes:
time: 47.9 us; the launch traced here: 47.3 us
  Pallas kernels  28.6 us (60%)
  local copies, waits for them, and re-layouts  16.3 us (34%)
  other arithmetic  1.62 us (3%)
  between operations  0.81 us (2%)
    pallas_call x1, Pallas kernels, one_kernel(): pl.pallas_call(functools.partial(step_kernel, half, bands), out_shape=[ja...  28.6 us
    unnamed x14, local copies, waits for them, and re-layouts  4.9 us
    reshape x4, local copies, waits for them, and re-layouts, to_kernel(): halves = field.reshape(8, 4, 2, 2, half).transpose(3, 1, 2, 0, 4)  4.46 us
    reshape x9, local copies, waits for them, and re-layouts, wind_rows(): field.reshape(4, 2, 2, half).transpose(0, 2, 1, 3).reshape(4, 4, half)  2.97 us

commit v1 on v0

--- a/solution.py
+++ b/solution.py
@@ -149,7 +149,7 @@
     lowest = 3 * length // 8 + 1
     forward = np.zeros((2, 2, padded, MODES), ml_dtypes.bfloat16)
     backward = np.zeros((2, 2, MODES, padded), ml_dtypes.bfloat16)
-    numbers = np.zeros((2, MODES), np.int32)
+    layout = []
     sample = np.arange(half)
     for parity in range(2):
         cosines = [m for m in range(lowest, nyquist + 1) if m % 2 == parity]
@@ -165,8 +165,8 @@
         for part, piece in enumerate((high, low)):
             forward[parity, part, :half, :count] = piece
             backward[parity, part, :count, :half] = piece.T
-        numbers[parity, :count] = waves
-    return forward, backward, numbers
+        layout.append((cosines[0], len(cosines), count))
+    return forward, backward, tuple(layout)
 
 
 def split_dot(rows, high, low):
@@ -196,34 +196,53 @@
 def step_kernel(
     half,
     bands,
-    tl,
-    adj,
-    winds,
-    ops,
-    counts,
-    mask,
+    layout,
+    cutoffs,
+    cost,
+    tl_hbm,
+    adj_hbm,
+    zonal_hbm,
+    merid_hbm,
+    vert_hbm,
+    state_hbm,
+    op_hbm,
+    remap_hbm,
     fwd_hbm,
     bwd_hbm,
     out_tl,
     out_adj,
+    tl,
+    adj,
+    zonal_raw,
+    merid_raw,
+    vert_raw,
+    state_raw,
+    op_raw,
+    remap_raw,
     fwd,
     bwd,
+    winds,
     qx,
     wext,
+    ah,
     acols,
     tbuf,
     tcols,
     aback,
     tback,
+    tband,
     abuf,
     mx,
     vx,
+    part,
+    spread,
     mats,
+    mask,
     send_sem,
     recv_sem,
     load_sem,
 ):
-    width = tl.shape[-1]
+    width = qx.shape[-1]
     tiles = width // LANES
     lev = lax.axis_index("lev")
     lat = lax.axis_index("lat")
@@ -232,9 +251,24 @@
     has_down = lat > 0
 
     loads = [
-        pltpu.make_async_copy(fwd_hbm, fwd, load_sem.at[0]),
-        pltpu.make_async_copy(bwd_hbm, bwd, load_sem.at[1]),
+        pltpu.make_async_copy(src, dst, load_sem.at[number])
+        for number, (src, dst) in enumerate(
+            [
+                (tl_hbm, tl),
+                (adj_hbm, adj),
+                (zonal_hbm, zonal_raw),
+                (merid_hbm, merid_raw),
+                (vert_hbm, vert_raw),
+                (state_hbm, state_raw),
+                (op_hbm, op_raw),
+                (remap_hbm, remap_raw),
+                (fwd_hbm, fwd),
+                (bwd_hbm, bwd),
+            ]
+        )
     ]
+    for load in loads:
+        load.start()
 
     barrier = pltpu.get_barrier_semaphore()
     pl.semaphore_signal(barrier, inc=1, device_id=(other, lat), device_id_type=MESH_IDS)
@@ -268,14 +302,14 @@
         )
 
     edge = 3 * other
-    lev_halo = remote(0, tl.at[:, edge], qx.at[:, 5 * lev, pl.ds(1, 2)], other, lat)
-    lat_up = remote(1, tl.at[:, :, 1], qx.at[:, pl.ds(1, 4), 0], lev, lat + 1)
-    lat_down = remote(2, tl.at[:, :, 0], qx.at[:, pl.ds(1, 4), 3], lev, lat - 1)
+    lev_halo = remote(0, qx.at[:, 1 + edge, pl.ds(1, 2)], qx.at[:, 5 * lev, pl.ds(1, 2)], other, lat)
+    lat_up = remote(1, qx.at[:, pl.ds(1, 4), 2], qx.at[:, pl.ds(1, 4), 0], lev, lat + 1)
+    lat_down = remote(2, qx.at[:, pl.ds(1, 4), 1], qx.at[:, pl.ds(1, 4), 3], lev, lat - 1)
     wind_halo = remote(3, winds.at[edge, pl.ds(8, 8)], wext, other, lat)
     mine = pl.ds(4 * lev, 4)
     theirs = pl.ds(4 * other, 4)
     adj_out_cols = [
-        remote(4 + i, adj.at[other, :, i], acols.at[mine, i], other, lat) for i in range(2)
+        remote(4 + i, ah.at[other, :, i], acols.at[mine, i], other, lat) for i in range(2)
     ]
     adj_in_bands = [
         remote(6 + i, aback.at[pl.ds(3 * other, 5), i], abuf.at[lev, :, i], other, lat)
@@ -285,11 +319,21 @@
         remote(8 + i, tbuf.at[other, :, i], tcols.at[mine, i], other, lat) for i in range(2)
     ]
     tl_in_bands = [
-        remote(10 + i, tback.at[theirs, i], out_tl.at[lev, :, i], other, lat) for i in range(2)
+        remote(10 + i, tback.at[theirs, i], tband.at[lev, :, i], other, lat) for i in range(2)
     ]
     merid_up = remote(12, mx.at[:, :, 2], mx.at[:, :, 0], lev, lat + 1)
     merid_down = remote(13, mx.at[:, :, 1], mx.at[:, :, 3], lev, lat - 1)
 
+    def halves(row):
+        first = jnp.concatenate([row[:, :half], jnp.zeros((8, width - half), F32)], axis=1)
+        second = jnp.concatenate([row[:, half:], jnp.zeros((8, width - half), F32)], axis=1)
+        return first, second
+
+    loads[0].wait()
+    for k in range(4):
+        for i in range(2):
+            for h, block in enumerate(halves(tl[:, k, i, :])):
+                qx[h, 1 + k, 1 + i] = block
     lev_halo.start()
 
     @pl.when(has_up)
@@ -300,11 +344,27 @@
     def _():
         lat_down.start()
 
+    for load in loads[1:6]:
+        load.wait()
+    blank = jnp.zeros((4, width - half), F32)
+    for k in range(4):
+        for first, raw in ((0, zonal_raw), (4, merid_raw), (8, vert_raw)):
+            for h in range(2):
+                for i in range(2):
+                    winds[k, first + 2 * h + i : first + 2 * h + i + 1, :half] = raw[
+                        k, i : i + 1, h * half : (h + 1) * half
+                    ]
+            winds[k, first : first + 4, half:] = blank
+        for l in range(2):
+            winds[k, 12 + 2 * l : 14 + 2 * l, :half] = state_raw[2 * k + l]
+        winds[k, 12:16, half:] = blank
     wind_halo.start()
-    for copy in adj_out_cols:
-        copy.start()
-    for load in loads:
-        load.start()
+    for i in range(2):
+        for k in range(4):
+            for h, block in enumerate(halves(adj[:, k, i, :])):
+                ah[h, k, i] = block
+        adj_out_cols[i].start()
+    acols[mine] = ah[lev]
 
     zeros = jnp.zeros((8, width), F32)
 
@@ -326,12 +386,25 @@
         for i in range(2):
             qx[h, 5 * lev, 1 + i] = zeros
             vx[h, 5 * lev, i] = zeros
-    qx[:, 1:5, 1:3] = tl[...]
-    acols[mine] = adj[lev]
-
-    table = ops[...]
-    for entry in range(128):
-        mats[entry] = jnp.broadcast_to(table[:, entry : entry + 1], (8, LANES))
+
+    for load in loads[6:8]:
+        load.wait()
+    for base, raw in ((0, op_raw), (64, remap_raw)):
+        for f in range(8):
+            table = raw[f]
+            for l in range(8):
+                at = (f * 8 + l) * 8
+                spread[at : at + 8, :] = jnp.broadcast_to(table[:, l : l + 1], (8, LANES))
+        for k in range(8):
+            for l in range(8):
+                mats[base + 8 * k + l] = spread[pl.ds(8 * l + k, 8, stride=64), :]
+
+    column = lax.broadcasted_iota(jnp.int32, (8, MODES), 1)
+    for parity, (first, cosines, count) in enumerate(layout):
+        number = first + 2 * jnp.where(column < cosines, column, column - cosines)
+        for i in range(2):
+            drop = jnp.logical_and(number > cutoffs[i], column < count)
+            mask[parity, i] = jnp.where(drop, 1.0, 0.0).astype(F32)
 
     lane = lax.broadcasted_iota(jnp.int32, (8, width), 1)
 
@@ -369,7 +442,7 @@
         return carry
 
     lax.fori_loop(0, 4, advect, 0)
-    for load in loads:
+    for load in loads[8:]:
         load.wait()
     filter_in_place(tbuf, 4, mask, fwd, bwd)
     for copy in tl_out_cols:
@@ -388,7 +461,7 @@
         return result
 
     def physics(src, dst, i, adjoint):
-        steps = counts[i]
+        steps = jnp.full((8, LANES), cost[i, 0], jnp.int32)
 
         def tile(t, carry):
             cols = pl.ds(pl.multiple_of(t * LANES, LANES), LANES)
@@ -429,7 +502,7 @@
         tl_out_cols[i].wait_recv()
         physics(tcols, tback, i, False)
         tl_in_bands[i].start()
-    out_tl[lev] = tback[mine]
+    tband[lev] = tback[mine]
 
     wind_halo.wait_recv()
     for i in range(2):
@@ -472,29 +545,37 @@
             z = [wind(winds[k, 2 * h + i : 2 * h + i + 1]) * p[h] for h in range(2)]
             for h in range(2):
                 total = lon_diff(z[h], z[1 - h]) + (vx[h, k + 2, i] - vx[h, k, i])
-                out_adj[h, k, i] = p[h] + 0.5 * total
+                part[h, k, i] = p[h] + 0.5 * total
         return carry
 
     lax.fori_loop(0, 4, zonal_parts, 0)
 
-    @pl.when(has_down)
-    def _():
-        merid_up.wait_recv()
-
-    @pl.when(has_up)
-    def _():
-        merid_down.wait_recv()
-
-    def add_merid(k, carry):
-        for h in range(2):
-            for i in range(2):
-                out_adj[h, k, i] = out_adj[h, k, i] + 0.5 * (mx[h, k, i + 2] - mx[h, k, i])
-        return carry
-
-    lax.fori_loop(0, 4, add_merid, 0)
+    def join(pair):
+        return jnp.concatenate([block[:, :half] for block in pair], axis=1)
 
     for copy in tl_in_bands:
         copy.wait_recv()
+    for k in range(4):
+        for i in range(2):
+            out_tl[:, k, i, :] = join([tband[h, k, i] for h in range(2)])
+
+    @pl.when(has_down)
+    def _():
+        merid_up.wait_recv()
+
+    @pl.when(has_up)
+    def _():
+        merid_down.wait_recv()
+
+    for k in range(4):
+        for i in range(2):
+            out_adj[:, k, i, :] = join(
+                [
+                    part[h, k, i] + 0.5 * (mx[h, k, i + 2] - mx[h, k, i])
+                    for h in range(2)
+                ]
+            )
+
     for copy in [lev_halo, wind_halo] + adj_out_cols + adj_in_bands + tl_out_cols + tl_in_bands:
         copy.wait_send()
 
@@ -524,79 +605,51 @@
     length = tl_pert.shape[3]
     half = length // 2
     padded = -(-half // LANES) * LANES
-    spare = padded - half
     bands = lax.axis_size("lat")
-    forward, backward, numbers = mode_tables(length, half, padded)
-
-    def to_kernel(field):
-        halves = field.reshape(8, 4, 2, 2, half).transpose(3, 1, 2, 0, 4)
-        return jnp.pad(halves, ((0, 0),) * 4 + ((0, spare),))
-
-    def from_kernel(field):
-        return field[..., :half].transpose(3, 1, 2, 0, 4).reshape(8, 4, 2, length)
-
-    def wind_rows(field):
-        return field.reshape(4, 2, 2, half).transpose(0, 2, 1, 3).reshape(4, 4, half)
-
-    winds = jnp.concatenate(
-        [
-            wind_rows(zonal_wind),
-            wind_rows(merid_wind),
-            wind_rows(vert_wind),
-            phys_state.reshape(4, 4, half),
-        ],
-        axis=1,
-    )
-    winds = jnp.pad(winds, ((0, 0), (0, 0), (0, spare)))
-    ops = jnp.concatenate([phys_op.reshape(8, 64), remap.reshape(8, 64)], axis=1)
-    counts = jnp.broadcast_to(column_cost[:, :, None], (2, 8, LANES))
-    drop = (jnp.asarray(numbers)[:, None, None, :] > cutoffs[None, :, None, None]).astype(F32)
-    mask = jnp.broadcast_to(drop, (2, 2, 8, MODES))
-
+    forward, backward, layout = mode_tables(length, half, padded)
     vmem = pl.BlockSpec(memory_space=pltpu.VMEM)
+    smem = pl.BlockSpec(memory_space=pltpu.SMEM)
     hbm = pl.BlockSpec(memory_space=pl.ANY)
     band_shape = (2, 4, 2, 8, padded)
     column_shape = (8, 2, 8, padded)
-    outs = pl.pallas_call(
-        functools.partial(step_kernel, half, bands),
-        out_shape=[jax.ShapeDtypeStruct(band_shape, F32)] * 2,
-        in_specs=[vmem] * 6 + [hbm] * 2,
+    fields = [tl_pert, adj_in, zonal_wind, merid_wind, vert_wind, phys_state, phys_op, remap]
+    return pl.pallas_call(
+        functools.partial(step_kernel, half, bands, layout),
+        out_shape=[jax.ShapeDtypeStruct(tl_pert.shape, F32)] * 2,
+        in_specs=[smem] * 2 + [hbm] * 10,
         out_specs=[vmem] * 2,
-        scratch_shapes=[
+        scratch_shapes=[pltpu.VMEM(field.shape, F32) for field in fields]
+        + [
             pltpu.VMEM(forward.shape, BF16),
             pltpu.VMEM(backward.shape, BF16),
+            pltpu.VMEM((4, 16, padded), F32),
             pltpu.VMEM((2, 6, 4, 8, padded), F32),
             pltpu.VMEM((8, padded), F32),
+            pltpu.VMEM(band_shape, F32),
             pltpu.VMEM(column_shape, F32),
             pltpu.VMEM(band_shape, F32),
             pltpu.VMEM(column_shape, F32),
             pltpu.VMEM(column_shape, F32),
             pltpu.VMEM(column_shape, F32),
+            pltpu.VMEM(band_shape, F32),
             pltpu.VMEM((2, 5, 2, 8, padded), F32),
             pltpu.VMEM((2, 4, 4, 8, padded), F32),
             pltpu.VMEM((2, 6, 2, 8, padded), F32),
+            pltpu.VMEM(band_shape, F32),
+            pltpu.VMEM((512, LANES), F32),
             pltpu.VMEM((128, 8, LANES), F32),
+            pltpu.VMEM((2, 2, 8, MODES), F32),
             pltpu.SemaphoreType.DMA((14,)),
             pltpu.SemaphoreType.DMA((14,)),
-            pltpu.SemaphoreType.DMA((2,)),
+            pltpu.SemaphoreType.DMA((10,)),
         ],
         compiler_params=pltpu.CompilerParams(
-            collective_id=0, has_side_effects=True, vmem_limit_bytes=40 * 1024 * 1024
+            collective_id=0, has_side_effects=True, vmem_limit_bytes=56 * 1024 * 1024
         ),
         cost_estimate=pl.CostEstimate(
             flops=10**9, bytes_accessed=8 * 10**6, transcendentals=0
         ),
-    )(
-        to_kernel(tl_pert),
-        to_kernel(adj_in),
-        winds,
-        ops,
-        counts,
-        mask,
-        jnp.asarray(forward),
-        jnp.asarray(backward),
-    )
-    return from_kernel(outs[0]), from_kernel(outs[1])
+    )(cutoffs, column_cost, *fields, jnp.asarray(forward), jnp.asarray(backward))
 
 
 def fits_kernel(mesh):

time: 47.9 us -> 36.1 us (0.75)
  local copies, waits for them, and re-layouts: 16.3 us -> 4.83 us
  Pallas kernels: 28.6 us -> 30.4 us
  other arithmetic: 1.62 us -> 0 us
    reshape x16 -> x0, local copies, waits for them, and re-layouts: 9.94 us -> none  [the longest x4 4.46 us: to_kernel(): halves = field.reshape(8, 4, 2, 2, half).transpose(3, 1, 2, 0, 4)]
    pallas_call x1, Pallas kernels: 28.6 us -> 30.4 us  [one_kernel(): pl.pallas_call(functools.partial(step_kernel, half, bands, layout), out_s...]
    broadcast_in_dim x2 -> x0, local copies, waits for them, and re-layouts: 1.34 us -> none  [the longest x1 0.73 us: one_kernel(): counts = jnp.broadcast_to(column_cost[:, :, None], (2, 8, LANES))]
    concatenate x2 -> x0, other arithmetic: 0.81 us -> none  [the longest x1 0.73 us: one_kernel(): jnp.concatenate([wind_rows(zonal_wind), wind_rows(merid_wind), wind_rows(...]
    convert_element_type x1 -> x0, other arithmetic: 0.81 us -> none  [one_kernel(): (jnp.asarray(numbers)[:, None, None, :] > cutoffs[None, :, None, None]).a...]
    unnamed x14 -> x3, local copies, waits for them, and re-layouts: 4.9 us -> 4.83 us
where the time goes in v1:
time: 36.1 us; the launch traced here: 35.9 us
  Pallas kernels  30.4 us (84%)
  local copies, waits for them, and re-layouts  4.83 us (13%)
  between operations  0.64 us (2%)
    pallas_call x1, Pallas kernels, one_kernel(): pl.pallas_call(functools.partial(step_kernel, half, bands, layout), out_s...  30.4 us
    unnamed x3, local copies, waits for them, and re-layouts  4.83 us

profile of v1, /device:TPU:1, one launch (start us, length us, event | category | flops | bytes accessed | tf_op | source)
XLA Modules:
  0.0 35.9 jit_solution(4029622441010197710)
XLA Ops:
  0.6 1.3 %copy.14.cost = s32[2,1]{1,0:T(2,128)} copy(s32[2,1]{0,1:T(1,128)} %param.21) | data formatting | bytes 16 | tf_op args[9]
  1.9 30.4 %shard_map.131 = (f32[8,4,2,1440]{3,2,1,0:T(2,128)}, f32[8,4,2,1440]{3,2,1,0:T(2,128)}) custom-call(s32[2]{0:T(128)} %cutoffs.1, s32[2,1]{1,0:T(2,128)} %copy.14.cost, f32[8,4,2,1440]{3,2,1,0:T(2,128)} %tl_hbm.1, f32[8,4,2,1440]{3,2,1,0:T(2,128)} %adj_hbm.1, f32[4,2,1440]{2,1,0:T(2,128)} %zonal_hbm.1, f32[4,2,1440]{2,1,0:T(2,128)} %merid_hbm.1, ...), custom_call_target="tpu_custom_call" | custom-call | flops 1000000000 | bytes 8000000 | tf_op jit(solution)/shard_map/pallas_call | solution.py:616
  32.4 1.8 %copy.17 = f32[8,4,2,1440]{3,2,1,0:T(2,128)} copy(f32[8,4,2,1440]{3,2,1,0:T(2,128)} %get-tuple-element.4) | data formatting | bytes 737280
  34.1 1.8 %copy.18 = f32[8,4,2,1440]{3,2,1,0:T(2,128)} copy(f32[8,4,2,1440]{3,2,1,0:T(2,128)} %get-tuple-element.5) | data formatting | bytes 737280

commit v2 on v1

--- a/solution.py
+++ b/solution.py
@@ -209,8 +209,8 @@
     remap_hbm,
     fwd_hbm,
     bwd_hbm,
-    out_tl,
-    out_adj,
+    tl_done,
+    adj_done,
     tl,
     adj,
     zonal_raw,
@@ -231,6 +231,8 @@
     aback,
     tback,
     tband,
+    out_tl,
+    out_adj,
     abuf,
     mx,
     vx,
@@ -302,7 +304,6 @@
         )
 
     edge = 3 * other
-    lev_halo = remote(0, qx.at[:, 1 + edge, pl.ds(1, 2)], qx.at[:, 5 * lev, pl.ds(1, 2)], other, lat)
     lat_up = remote(1, qx.at[:, pl.ds(1, 4), 2], qx.at[:, pl.ds(1, 4), 0], lev, lat + 1)
     lat_down = remote(2, qx.at[:, pl.ds(1, 4), 1], qx.at[:, pl.ds(1, 4), 3], lev, lat - 1)
     wind_halo = remote(3, winds.at[edge, pl.ds(8, 8)], wext, other, lat)
@@ -316,7 +317,7 @@
         for i in range(2)
     ]
     tl_out_cols = [
-        remote(8 + i, tbuf.at[other, :, i], tcols.at[mine, i], other, lat) for i in range(2)
+        remote(8 + i, tbuf.at[other, :, i], tcols.at[lev, :, i], other, lat) for i in range(2)
     ]
     tl_in_bands = [
         remote(10 + i, tback.at[theirs, i], tband.at[lev, :, i], other, lat) for i in range(2)
@@ -329,22 +330,33 @@
         second = jnp.concatenate([row[:, half:], jnp.zeros((8, width - half), F32)], axis=1)
         return first, second
 
+    loads[1].wait()
+    for i in range(2):
+        for k in range(4):
+            for h, block in enumerate(halves(adj[:, k, i, :])):
+                ah[h, k, i] = block
+        adj_out_cols[i].start()
+
     loads[0].wait()
-    for k in range(4):
-        for i in range(2):
+
+    def to_halves(i):
+        for k in range(4):
             for h, block in enumerate(halves(tl[:, k, i, :])):
                 qx[h, 1 + k, 1 + i] = block
-    lev_halo.start()
+
+    to_halves(1)
 
     @pl.when(has_up)
     def _():
         lat_up.start()
 
+    to_halves(0)
+
     @pl.when(has_down)
     def _():
         lat_down.start()
 
-    for load in loads[1:6]:
+    for load in loads[2:6]:
         load.wait()
     blank = jnp.zeros((4, width - half), F32)
     for k in range(4):
@@ -359,11 +371,6 @@
             winds[k, 12 + 2 * l : 14 + 2 * l, :half] = state_raw[2 * k + l]
         winds[k, 12:16, half:] = blank
     wind_halo.start()
-    for i in range(2):
-        for k in range(4):
-            for h, block in enumerate(halves(adj[:, k, i, :])):
-                ah[h, k, i] = block
-        adj_out_cols[i].start()
     acols[mine] = ah[lev]
 
     zeros = jnp.zeros((8, width), F32)
@@ -384,7 +391,8 @@
 
     for h in range(2):
         for i in range(2):
-            qx[h, 5 * lev, 1 + i] = zeros
+            qx[h, 0, 1 + i] = zeros
+            qx[h, 5, 1 + i] = zeros
             vx[h, 5 * lev, i] = zeros
 
     for load in loads[6:8]:
@@ -416,7 +424,58 @@
         before = jnp.where(lane == 0, across[:, half - 1 : half], pltpu.roll(z, 1, 1))
         return after - before
 
-    lev_halo.wait_recv()
+    def product(base, transposed, vec):
+        result = []
+        for k in range(8):
+            terms = [
+                mats[base + (8 * l + k if transposed else 8 * k + l)] * vec[l] for l in range(8)
+            ]
+            while len(terms) > 1:
+                terms = [a + b for a, b in zip(terms[::2], terms[1::2])]
+            result.append(terms[0])
+        return result
+
+    def physics(src, dst, i, adjoint):
+        steps = jnp.full((8, LANES), cost[i], jnp.int32)
+
+        def tile(t, carry):
+            cols = pl.ds(pl.multiple_of(t * LANES, LANES), LANES)
+            state = [
+                jnp.broadcast_to(
+                    winds[l // 2, 12 + 2 * (l % 2) + i : 13 + 2 * (l % 2) + i, cols], (8, LANES)
+                )
+                for l in range(8)
+            ]
+            if adjoint:
+                vec = [src[l, i, :, cols] for l in range(8)]
+            else:
+                low = [src[0, l, i, :, cols] for l in range(5)]
+                high = [src[1, l, i, :, cols] for l in range(5)]
+                both = [low[3] + high[0], low[4] + high[1]]
+                vec = product(64, False, low[:3] + both + high[2:])
+
+            def sub_step(s, vec):
+                if adjoint:
+                    new = [d * v for d, v in zip(state, product(0, True, vec))]
+                else:
+                    new = product(0, False, [d * v for d, v in zip(state, vec)])
+                active = s < steps
+                return [jnp.where(active, n, v) for n, v in zip(new, vec)]
+
+            vec = lax.fori_loop(0, SUBS, sub_step, vec)
+            if adjoint:
+                vec = product(64, True, vec)
+            for k in range(8):
+                dst[k, i, :, cols] = vec[k]
+            return carry
+
+        lax.fori_loop(0, tiles, tile, 0)
+
+    for i in range(2):
+        adj_out_cols[i].wait_recv()
+        physics(acols, aback, i, True)
+        adj_in_bands[i].start()
+    abuf[lev] = aback[pl.ds(3 * lev, 5)]
 
     @pl.when(has_down)
     def _():
@@ -438,73 +497,24 @@
                 vert = wind(winds[k, 8 + row : 9 + row]) * (
                     qx[h, k + 2, i + 1] - qx[h, k, i + 1]
                 )
-                tbuf[h, k, i] = q - 0.5 * (zonal + merid + vert)
+                tbuf[h, k + lev, i] = q - 0.5 * (zonal + merid + vert)
         return carry
 
     lax.fori_loop(0, 4, advect, 0)
+
+    wind_halo.wait_recv()
+    sign = 0.5 - lev.astype(F32)
+    for h in range(2):
+        for i in range(2):
+            row = 2 * h + i
+            tbuf[h, 4 * other, i] = sign * (wind(wext[row : row + 1]) * qx[h, 1 + edge, 1 + i])
     for load in loads[8:]:
         load.wait()
-    filter_in_place(tbuf, 4, mask, fwd, bwd)
+    filter_in_place(tbuf, 5, mask, fwd, bwd)
     for copy in tl_out_cols:
         copy.start()
-    tcols[mine] = tbuf[lev]
-
-    def product(base, transposed, vec):
-        result = []
-        for k in range(8):
-            terms = [
-                mats[base + (8 * l + k if transposed else 8 * k + l)] * vec[l] for l in range(8)
-            ]
-            while len(terms) > 1:
-                terms = [a + b for a, b in zip(terms[::2], terms[1::2])]
-            result.append(terms[0])
-        return result
-
-    def physics(src, dst, i, adjoint):
-        steps = jnp.full((8, LANES), cost[i, 0], jnp.int32)
-
-        def tile(t, carry):
-            cols = pl.ds(pl.multiple_of(t * LANES, LANES), LANES)
-            state = [
-                jnp.broadcast_to(
-                    winds[l // 2, 12 + 2 * (l % 2) + i : 13 + 2 * (l % 2) + i, cols], (8, LANES)
-                )
-                for l in range(8)
-            ]
-            vec = [src[l, i, :, cols] for l in range(8)]
-            if not adjoint:
-                vec = product(64, False, vec)
-
-            def sub_step(s, vec):
-                if adjoint:
-                    new = [d * v for d, v in zip(state, product(0, True, vec))]
-                else:
-                    new = product(0, False, [d * v for d, v in zip(state, vec)])
-                active = s < steps
-                return [jnp.where(active, n, v) for n, v in zip(new, vec)]
-
-            vec = lax.fori_loop(0, SUBS, sub_step, vec)
-            if adjoint:
-                vec = product(64, True, vec)
-            for k in range(8):
-                dst[k, i, :, cols] = vec[k]
-            return carry
-
-        lax.fori_loop(0, tiles, tile, 0)
-
-    for i in range(2):
-        adj_out_cols[i].wait_recv()
-        physics(acols, aback, i, True)
-        adj_in_bands[i].start()
-    abuf[lev] = aback[pl.ds(3 * lev, 5)]
-
-    for i in range(2):
-        tl_out_cols[i].wait_recv()
-        physics(tcols, tback, i, False)
-        tl_in_bands[i].start()
-    tband[lev] = tback[mine]
-
-    wind_halo.wait_recv()
+    tcols[lev] = tbuf[lev]
+
     for i in range(2):
         adj_in_bands[i].wait_recv()
     filter_in_place(abuf, 5, mask, fwd, bwd)
@@ -550,14 +560,14 @@
 
     lax.fori_loop(0, 4, zonal_parts, 0)
 
+    for i in range(2):
+        tl_out_cols[i].wait_recv()
+        physics(tcols, tback, i, False)
+        tl_in_bands[i].start()
+    tband[lev] = tback[mine]
+
     def join(pair):
         return jnp.concatenate([block[:, :half] for block in pair], axis=1)
-
-    for copy in tl_in_bands:
-        copy.wait_recv()
-    for k in range(4):
-        for i in range(2):
-            out_tl[:, k, i, :] = join([tband[h, k, i] for h in range(2)])
 
     @pl.when(has_down)
     def _():
@@ -575,8 +585,18 @@
                     for h in range(2)
                 ]
             )
-
-    for copy in [lev_halo, wind_halo] + adj_out_cols + adj_in_bands + tl_out_cols + tl_in_bands:
+    adj_store = pltpu.make_async_copy(out_adj, adj_done, load_sem.at[10])
+    adj_store.start()
+
+    for copy in tl_in_bands:
+        copy.wait_recv()
+    for k in range(4):
+        for i in range(2):
+            out_tl[:, k, i, :] = join([tband[h, k, i] for h in range(2)])
+    tl_store = pltpu.make_async_copy(out_tl, tl_done, load_sem.at[11])
+    tl_store.start()
+
+    for copy in [wind_halo] + adj_out_cols + adj_in_bands + tl_out_cols + tl_in_bands:
         copy.wait_send()
 
     @pl.when(has_up)
@@ -588,6 +608,20 @@
     def _():
         lat_down.wait_send()
         merid_down.wait_send()
+
+    adj_store.wait()
+    tl_store.wait()
+
+
+def hand_over(first, second, first_out, second_out, sems):
+    copies = [
+        pltpu.make_async_copy(first, first_out, sems.at[0]),
+        pltpu.make_async_copy(second, second_out, sems.at[1]),
+    ]
+    for copy in copies:
+        copy.start()
+    for copy in copies:
+        copy.wait()
 
 
 def one_kernel(
@@ -607,17 +641,17 @@
     padded = -(-half // LANES) * LANES
     bands = lax.axis_size("lat")
     forward, backward, layout = mode_tables(length, half, padded)
-    vmem = pl.BlockSpec(memory_space=pltpu.VMEM)
     smem = pl.BlockSpec(memory_space=pltpu.SMEM)
     hbm = pl.BlockSpec(memory_space=pl.ANY)
     band_shape = (2, 4, 2, 8, padded)
+    edged_shape = (2, 5, 2, 8, padded)
     column_shape = (8, 2, 8, padded)
     fields = [tl_pert, adj_in, zonal_wind, merid_wind, vert_wind, phys_state, phys_op, remap]
-    return pl.pallas_call(
+    done = pl.pallas_call(
         functools.partial(step_kernel, half, bands, layout),
         out_shape=[jax.ShapeDtypeStruct(tl_pert.shape, F32)] * 2,
         in_specs=[smem] * 2 + [hbm] * 10,
-        out_specs=[vmem] * 2,
+        out_specs=[hbm] * 2,
         scratch_shapes=[pltpu.VMEM(field.shape, F32) for field in fields]
         + [
             pltpu.VMEM(forward.shape, BF16),
@@ -627,12 +661,14 @@
             pltpu.VMEM((8, padded), F32),
             pltpu.VMEM(band_shape, F32),
             pltpu.VMEM(column_shape, F32),
-            pltpu.VMEM(band_shape, F32),
-            pltpu.VMEM(column_shape, F32),
+            pltpu.VMEM(edged_shape, F32),
+            pltpu.VMEM(edged_shape, F32),
             pltpu.VMEM(column_shape, F32),
             pltpu.VMEM(column_shape, F32),
             pltpu.VMEM(band_shape, F32),
-            pltpu.VMEM((2, 5, 2, 8, padded), F32),
+            pltpu.VMEM(tl_pert.shape, F32),
+            pltpu.VMEM(tl_pert.shape, F32),
+            pltpu.VMEM(edged_shape, F32),
             pltpu.VMEM((2, 4, 4, 8, padded), F32),
             pltpu.VMEM((2, 6, 2, 8, padded), F32),
             pltpu.VMEM(band_shape, F32),
@@ -641,7 +677,7 @@
             pltpu.VMEM((2, 2, 8, MODES), F32),
             pltpu.SemaphoreType.DMA((14,)),
             pltpu.SemaphoreType.DMA((14,)),
-            pltpu.SemaphoreType.DMA((10,)),
+            pltpu.SemaphoreType.DMA((12,)),
         ],
         compiler_params=pltpu.CompilerParams(
             collective_id=0, has_side_effects=True, vmem_limit_bytes=56 * 1024 * 1024
@@ -649,7 +685,15 @@
         cost_estimate=pl.CostEstimate(
             flops=10**9, bytes_accessed=8 * 10**6, transcendentals=0
         ),
-    )(cutoffs, column_cost, *fields, jnp.asarray(forward), jnp.asarray(backward))
+    )(cutoffs, column_cost[:, 0], *fields, jnp.asarray(forward), jnp.asarray(backward))
+    return pl.pallas_call(
+        hand_over,
+        out_shape=[jax.ShapeDtypeStruct(tl_pert.shape, F32)] * 2,
+        in_specs=[hbm] * 2,
+        out_specs=[hbm] * 2,
+        scratch_shapes=[pltpu.SemaphoreType.DMA((2,))],
+        compiler_params=pltpu.CompilerParams(vmem_limit_bytes=56 * 1024 * 1024),
+    )(*done)
 
 
 def fits_kernel(mesh):

time: 36.1 us -> 54.2 us (1.50)
  the two profiles are of different devices: /device:TPU:1 before, /device:TPU:0 now
where the time goes in v2:
time: 54.2 us; the launch traced here: 54.1 us
  Pallas kernels  53.4 us (99%)
  between operations  0.64 us (1%)
    pallas_call x1, Pallas kernels, one_kernel(): pl.pallas_call(functools.partial(step_kernel, half, bands, layout), out_s...  28.5 us
    pallas_call x1, Pallas kernels, one_kernel(): pl.pallas_call(hand_over, out_shape=[jax.ShapeDtypeStruct(tl_pert.shape,...  24.9 us

profile of v2, /device:TPU:0, one launch (start us, length us, event | category | flops | bytes accessed | tf_op | source)
XLA Modules:
  0.0 54.1 jit_solution(10377299592260960126)
XLA Ops:
  0.6 28.5 %shard_map.131 = (f32[8,4,2,1440]{3,2,1,0:T(2,128)}, f32[8,4,2,1440]{3,2,1,0:T(2,128)}) custom-call(s32[2]{0:T(128)} %cutoffs.1, s32[2]{0:T(128)} %bitcast.1, f32[8,4,2,1440]{3,2,1,0:T(2,128)} %tl_hbm.1, f32[8,4,2,1440]{3,2,1,0:T(2,128)} %adj_hbm.1, f32[4,2,1440]{2,1,0:T(2,128)} %zonal_hbm.1, f32[4,2,1440]{2,1,0:T(2,128)} %merid_hbm.1, ...), custom_call_target="tpu_custom_call" | custom-call | flops 1000000000 | bytes 8000000 | tf_op jit(solution)/shard_map/pallas_call | solution.py:650
  29.1 24.9 %shard_map.132 = (f32[8,4,2,1440]{3,2,1,0:T(2,128)}, f32[8,4,2,1440]{3,2,1,0:T(2,128)}) custom-call(f32[8,4,2,1440]{3,2,1,0:T(2,128)} %get-tuple-element.4.first, f32[8,4,2,1440]{3,2,1,0:T(2,128)} %get-tuple-element.5.second), custom_call_target="tpu_custom_call" | custom-call | tf_op jit(solution)/shard_map/pallas_call | solution.py:689

commit v3 on v2

--- a/solution.py
+++ b/solution.py
@@ -613,14 +613,18 @@
     tl_store.wait()
 
 
-def hand_over(first, second, first_out, second_out, sems):
-    copies = [
-        pltpu.make_async_copy(first, first_out, sems.at[0]),
-        pltpu.make_async_copy(second, second_out, sems.at[1]),
+def hand_over(first, second, first_out, second_out, first_held, second_held, sems):
+    pairs = ((first, first_held, first_out), (second, second_held, second_out))
+    inward = [pltpu.make_async_copy(src, held, sems.at[n]) for n, (src, held, _) in enumerate(pairs)]
+    outward = [
+        pltpu.make_async_copy(held, dst, sems.at[2 + n]) for n, (_, held, dst) in enumerate(pairs)
     ]
-    for copy in copies:
+    for copy in inward:
         copy.start()
-    for copy in copies:
+    for arrived, copy in zip(inward, outward):
+        arrived.wait()
+        copy.start()
+    for copy in outward:
         copy.wait()
 
 
@@ -691,7 +695,7 @@
         out_shape=[jax.ShapeDtypeStruct(tl_pert.shape, F32)] * 2,
         in_specs=[hbm] * 2,
         out_specs=[hbm] * 2,
-        scratch_shapes=[pltpu.SemaphoreType.DMA((2,))],
+        scratch_shapes=[pltpu.VMEM(tl_pert.shape, F32)] * 2 + [pltpu.SemaphoreType.DMA((4,))],
         compiler_params=pltpu.CompilerParams(vmem_limit_bytes=56 * 1024 * 1024),
     )(*done)
 

time: 54.2 us -> 31.2 us (0.58)
  Pallas kernels: 53.4 us -> 30.4 us
    pallas_call x1, Pallas kernels: 24.9 us -> 1.91 us  [one_kernel(): pl.pallas_call(hand_over, out_shape=[jax.ShapeDtypeStruct(tl_pert.shape,...]
where the time goes in v3:
time: 31.2 us; the launch traced here: 31 us
  Pallas kernels  30.4 us (97%)
  between operations  0.64 us (2%)
    pallas_call x1, Pallas kernels, one_kernel(): pl.pallas_call(functools.partial(step_kernel, half, bands, layout), out_s...  28.5 us
    pallas_call x1, Pallas kernels, one_kernel(): pl.pallas_call(hand_over, out_shape=[jax.ShapeDtypeStruct(tl_pert.shape,...  1.91 us

profile of v3, /device:TPU:0, one launch (start us, length us, event | category | flops | bytes accessed | tf_op | source)
XLA Modules:
  0.0 31.0 jit_solution(13616472924383247293)
XLA Ops:
  0.6 28.5 %shard_map.131 = (f32[8,4,2,1440]{3,2,1,0:T(2,128)}, f32[8,4,2,1440]{3,2,1,0:T(2,128)}) custom-call(s32[2]{0:T(128)} %cutoffs.1, s32[2]{0:T(128)} %bitcast.1, f32[8,4,2,1440]{3,2,1,0:T(2,128)} %tl_hbm.1, f32[8,4,2,1440]{3,2,1,0:T(2,128)} %adj_hbm.1, f32[4,2,1440]{2,1,0:T(2,128)} %zonal_hbm.1, f32[4,2,1440]{2,1,0:T(2,128)} %merid_hbm.1, ...), custom_call_target="tpu_custom_call" | custom-call | flops 1000000000 | bytes 8000000 | tf_op jit(solution)/shard_map/pallas_call | solution.py:654
  29.1 1.9 %shard_map.132 = (f32[8,4,2,1440]{3,2,1,0:T(2,128)}, f32[8,4,2,1440]{3,2,1,0:T(2,128)}) custom-call(f32[8,4,2,1440]{3,2,1,0:T(2,128)} %get-tuple-element.4.first, f32[8,4,2,1440]{3,2,1,0:T(2,128)} %get-tuple-element.5.second), custom_call_target="tpu_custom_call" | custom-call | tf_op jit(solution)/shard_map/pallas_call | solution.py:693

commit v4 on v2

--- a/solution.py
+++ b/solution.py
@@ -209,8 +209,8 @@
     remap_hbm,
     fwd_hbm,
     bwd_hbm,
-    tl_done,
-    adj_done,
+    out_tl,
+    out_adj,
     tl,
     adj,
     zonal_raw,
@@ -231,12 +231,10 @@
     aback,
     tback,
     tband,
-    out_tl,
-    out_adj,
     abuf,
     mx,
     vx,
-    part,
+    partial,
     spread,
     mats,
     mask,
@@ -269,8 +267,8 @@
             ]
         )
     ]
-    for load in loads:
-        load.start()
+    for number in (1, 0, 2, 3, 4, 5, 6, 7):
+        loads[number].start()
 
     barrier = pltpu.get_barrier_semaphore()
     pl.semaphore_signal(barrier, inc=1, device_id=(other, lat), device_id_type=MESH_IDS)
@@ -310,20 +308,30 @@
     mine = pl.ds(4 * lev, 4)
     theirs = pl.ds(4 * other, 4)
     adj_out_cols = [
-        remote(4 + i, ah.at[other, :, i], acols.at[mine, i], other, lat) for i in range(2)
+        remote(14 + i, ah.at[other, :, i], acols.at[mine, i], other, lat) for i in range(2)
     ]
+    pieces = [(i, pl.ds(part * width // 2, width // 2)) for i in range(2) for part in range(2)]
     adj_in_bands = [
-        remote(6 + i, aback.at[pl.ds(3 * other, 5), i], abuf.at[lev, :, i], other, lat)
-        for i in range(2)
+        remote(
+            4 + number,
+            aback.at[pl.ds(3 * other, 5), i, :, cols],
+            abuf.at[lev, :, i, :, cols],
+            other,
+            lat,
+        )
+        for number, (i, cols) in enumerate(pieces)
     ]
     tl_out_cols = [
         remote(8 + i, tbuf.at[other, :, i], tcols.at[lev, :, i], other, lat) for i in range(2)
     ]
     tl_in_bands = [
-        remote(10 + i, tback.at[theirs, i], tband.at[lev, :, i], other, lat) for i in range(2)
+        remote(
+            10 + number, tback.at[theirs, i, :, cols], tband.at[lev, :, i, :, cols], other, lat
+        )
+        for number, (i, cols) in enumerate(pieces)
     ]
-    merid_up = remote(12, mx.at[:, :, 2], mx.at[:, :, 0], lev, lat + 1)
-    merid_down = remote(13, mx.at[:, :, 1], mx.at[:, :, 3], lev, lat - 1)
+    merid_up = remote(0, mx.at[:, :, 2], mx.at[:, :, 0], lev, lat + 1)
+    merid_down = remote(16, mx.at[:, :, 1], mx.at[:, :, 3], lev, lat - 1)
 
     def halves(row):
         first = jnp.concatenate([row[:, :half], jnp.zeros((8, width - half), F32)], axis=1)
@@ -338,6 +346,8 @@
         adj_out_cols[i].start()
 
     loads[0].wait()
+    for load in loads[8:]:
+        load.start()
 
     def to_halves(i):
         for k in range(4):
@@ -435,7 +445,7 @@
             result.append(terms[0])
         return result
 
-    def physics(src, dst, i, adjoint):
+    def physics(src, dst, i, part, adjoint):
         steps = jnp.full((8, LANES), cost[i], jnp.int32)
 
         def tile(t, carry):
@@ -469,12 +479,13 @@
                 dst[k, i, :, cols] = vec[k]
             return carry
 
-        lax.fori_loop(0, tiles, tile, 0)
+        lax.fori_loop(part * tiles // 2, (part + 1) * tiles // 2, tile, 0)
 
     for i in range(2):
         adj_out_cols[i].wait_recv()
-        physics(acols, aback, i, True)
-        adj_in_bands[i].start()
+        for part in range(2):
+            physics(acols, aback, i, part, True)
+            adj_in_bands[2 * i + part].start()
     abuf[lev] = aback[pl.ds(3 * lev, 5)]
 
     @pl.when(has_down)
@@ -515,8 +526,8 @@
         copy.start()
     tcols[lev] = tbuf[lev]
 
-    for i in range(2):
-        adj_in_bands[i].wait_recv()
+    for copy in adj_in_bands:
+        copy.wait_recv()
     filter_in_place(abuf, 5, mask, fwd, bwd)
 
     def merid_parts(k, carry):
@@ -555,15 +566,16 @@
             z = [wind(winds[k, 2 * h + i : 2 * h + i + 1]) * p[h] for h in range(2)]
             for h in range(2):
                 total = lon_diff(z[h], z[1 - h]) + (vx[h, k + 2, i] - vx[h, k, i])
-                part[h, k, i] = p[h] + 0.5 * total
+                partial[h, k, i] = p[h] + 0.5 * total
         return carry
 
     lax.fori_loop(0, 4, zonal_parts, 0)
 
     for i in range(2):
         tl_out_cols[i].wait_recv()
-        physics(tcols, tback, i, False)
-        tl_in_bands[i].start()
+        for part in range(2):
+            physics(tcols, tback, i, part, False)
+            tl_in_bands[2 * i + part].start()
     tband[lev] = tback[mine]
 
     def join(pair):
@@ -581,20 +593,16 @@
         for i in range(2):
             out_adj[:, k, i, :] = join(
                 [
-                    part[h, k, i] + 0.5 * (mx[h, k, i + 2] - mx[h, k, i])
+                    partial[h, k, i] + 0.5 * (mx[h, k, i + 2] - mx[h, k, i])
                     for h in range(2)
                 ]
             )
-    adj_store = pltpu.make_async_copy(out_adj, adj_done, load_sem.at[10])
-    adj_store.start()
-
-    for copy in tl_in_bands:
-        copy.wait_recv()
-    for k in range(4):
-        for i in range(2):
+
+    for i in range(2):
+        for copy in tl_in_bands[2 * i : 2 * i + 2]:
+            copy.wait_recv()
+        for k in range(4):
             out_tl[:, k, i, :] = join([tband[h, k, i] for h in range(2)])
-    tl_store = pltpu.make_async_copy(out_tl, tl_done, load_sem.at[11])
-    tl_store.start()
 
     for copy in [wind_halo] + adj_out_cols + adj_in_bands + tl_out_cols + tl_in_bands:
         copy.wait_send()
@@ -608,9 +616,6 @@
     def _():
         lat_down.wait_send()
         merid_down.wait_send()
-
-    adj_store.wait()
-    tl_store.wait()
 
 
 def hand_over(first, second, first_out, second_out, sems):
@@ -641,6 +646,7 @@
     padded = -(-half // LANES) * LANES
     bands = lax.axis_size("lat")
     forward, backward, layout = mode_tables(length, half, padded)
+    vmem = pl.BlockSpec(memory_space=pltpu.VMEM)
     smem = pl.BlockSpec(memory_space=pltpu.SMEM)
     hbm = pl.BlockSpec(memory_space=pl.ANY)
     band_shape = (2, 4, 2, 8, padded)
@@ -649,9 +655,9 @@
     fields = [tl_pert, adj_in, zonal_wind, merid_wind, vert_wind, phys_state, phys_op, remap]
     done = pl.pallas_call(
         functools.partial(step_kernel, half, bands, layout),
-        out_shape=[jax.ShapeDtypeStruct(tl_pert.shape, F32)] * 2,
+        out_shape=[pltpu.VMEM(tl_pert.shape, F32)] * 2,
         in_specs=[smem] * 2 + [hbm] * 10,
-        out_specs=[hbm] * 2,
+        out_specs=[vmem] * 2,
         scratch_shapes=[pltpu.VMEM(field.shape, F32) for field in fields]
         + [
             pltpu.VMEM(forward.shape, BF16),
@@ -666,8 +672,6 @@
             pltpu.VMEM(column_shape, F32),
             pltpu.VMEM(column_shape, F32),
             pltpu.VMEM(band_shape, F32),
-            pltpu.VMEM(tl_pert.shape, F32),
-            pltpu.VMEM(tl_pert.shape, F32),
             pltpu.VMEM(edged_shape, F32),
             pltpu.VMEM((2, 4, 4, 8, padded), F32),
             pltpu.VMEM((2, 6, 2, 8, padded), F32),
@@ -675,9 +679,9 @@
             pltpu.VMEM((512, LANES), F32),
             pltpu.VMEM((128, 8, LANES), F32),
             pltpu.VMEM((2, 2, 8, MODES), F32),
-            pltpu.SemaphoreType.DMA((14,)),
-            pltpu.SemaphoreType.DMA((14,)),
-            pltpu.SemaphoreType.DMA((12,)),
+            pltpu.SemaphoreType.DMA((17,)),
+            pltpu.SemaphoreType.DMA((17,)),
+            pltpu.SemaphoreType.DMA((10,)),
         ],
         compiler_params=pltpu.CompilerParams(
             collective_id=0, has_side_effects=True, vmem_limit_bytes=56 * 1024 * 1024
@@ -689,10 +693,9 @@
     return pl.pallas_call(
         hand_over,
         out_shape=[jax.ShapeDtypeStruct(tl_pert.shape, F32)] * 2,
-        in_specs=[hbm] * 2,
+        in_specs=[vmem] * 2,
         out_specs=[hbm] * 2,
         scratch_shapes=[pltpu.SemaphoreType.DMA((2,))],
-        compiler_params=pltpu.CompilerParams(vmem_limit_bytes=56 * 1024 * 1024),
     )(*done)
 
 

time: 54.2 us -> 31 us (0.57)
  Pallas kernels: 53.4 us -> 28.7 us
  local copies, waits for them, and re-layouts: 0 us -> 1.5 us
    pallas_call x1, Pallas kernels: 24.9 us -> 2 us  [one_kernel(): pl.pallas_call(hand_over, out_shape=[jax.ShapeDtypeStruct(tl_pert.shape,...]
    pallas_call x1, Pallas kernels: 28.5 us -> 26.7 us  [one_kernel(): pl.pallas_call(functools.partial(step_kernel, half, bands, layout), out_s...]
    unnamed x0 -> x4, local copies, waits for them, and re-layouts: none -> 1.5 us
where the time goes in v4:
time: 31 us; the launch traced here: 30.9 us
  Pallas kernels  28.7 us (93%)
  local copies, waits for them, and re-layouts  1.5 us (5%)
  between operations  0.65 us (2%)
    pallas_call x1, Pallas kernels, one_kernel(): pl.pallas_call(functools.partial(step_kernel, half, bands, layout), out_s...  26.7 us
    pallas_call x1, Pallas kernels, one_kernel(): pl.pallas_call(hand_over, out_shape=[jax.ShapeDtypeStruct(tl_pert.shape,...  2 us
    unnamed x4, local copies, waits for them, and re-layouts  1.5 us

profile of v4, /device:TPU:0, one launch (start us, length us, event | category | flops | bytes accessed | tf_op | source)
XLA Modules:
  0.0 30.9 jit_solution(8341099231190220469)
XLA Ops:
  0.6 26.7 %shard_map.131 = (f32[8,4,2,1440]{3,2,1,0:T(2,128)S(1)}, f32[8,4,2,1440]{3,2,1,0:T(2,128)S(1)}) custom-call(s32[2]{0:T(128)} %cutoffs.1, s32[2]{0:T(128)} %bitcast.1, f32[8,4,2,1440]{3,2,1,0:T(2,128)} %tl_hbm.1, f32[8,4,2,1440]{3,2,1,0:T(2,128)} %adj_hbm.1, f32[4,2,1440]{2,1,0:T(2,128)} %zonal_hbm.1, f32[4,2,1440]{2,1,0:T(2,128)} %merid_hbm.1, ...), custom_call_target="tpu_custom_call" | custom-call | flops 1000000000 | bytes 8000000 | tf_op jit(solution)/shard_map/pallas_call | solution.py:656
  27.4 0.0 copy-start
  27.4 0.7 %copy-done = f32[8,4,2,1440]{3,2,1,0:T(2,128)} copy-done((f32[8,4,2,1440]{3,2,1,0:T(2,128)}, f32[8,4,2,1440]{3,2,1,0:T(2,128)S(1)}, u32[]{:S(2)}) %copy-start) | copy-done | bytes 368664
  28.1 0.0 copy-start.1
  28.1 0.7 %copy-done.1 = f32[8,4,2,1440]{3,2,1,0:T(2,128)} copy-done((f32[8,4,2,1440]{3,2,1,0:T(2,128)}, f32[8,4,2,1440]{3,2,1,0:T(2,128)S(1)}, u32[]{:S(2)}) %copy-start.1) | copy-done | bytes 368664
  28.9 2.0 %shard_map.132 = (f32[8,4,2,1440]{3,2,1,0:T(2,128)}, f32[8,4,2,1440]{3,2,1,0:T(2,128)}) custom-call(f32[8,4,2,1440]{3,2,1,0:T(2,128)} %copy-done, f32[8,4,2,1440]{3,2,1,0:T(2,128)} %copy-done.1), custom_call_target="tpu_custom_call" | custom-call | tf_op jit(solution)/shard_map/pallas_call | solution.py:693
Async XLA Ops:
  27.4 0.8 %copy-start = (f32[8,4,2,1440]{3,2,1,0:T(2,128)}, f32[8,4,2,1440]{3,2,1,0:T(2,128)S(1)}, u32[]{:S(2)}) copy-start(f32[8,4,2,1440]{3,2,1,0:T(2,128)S(1)} %get-tuple-element.4.first) | copy-start | bytes 1105924
  28.1 0.7 %copy-start.1 = (f32[8,4,2,1440]{3,2,1,0:T(2,128)}, f32[8,4,2,1440]{3,2,1,0:T(2,128)S(1)}, u32[]{:S(2)}) copy-start(f32[8,4,2,1440]{3,2,1,0:T(2,128)S(1)} %get-tuple-element.5.second) | copy-start | bytes 1105924

commit v5 on v4

--- a/solution.py
+++ b/solution.py
@@ -684,7 +684,7 @@
             pltpu.SemaphoreType.DMA((10,)),
         ],
         compiler_params=pltpu.CompilerParams(
-            collective_id=0, has_side_effects=True, vmem_limit_bytes=56 * 1024 * 1024
+            collective_id=0, has_side_effects=True, vmem_limit_bytes=48 * 1024 * 1024
         ),
         cost_estimate=pl.CostEstimate(
             flops=10**9, bytes_accessed=8 * 10**6, transcendentals=0
@@ -693,9 +693,10 @@
     return pl.pallas_call(
         hand_over,
         out_shape=[jax.ShapeDtypeStruct(tl_pert.shape, F32)] * 2,
-        in_specs=[vmem] * 2,
+        in_specs=[hbm] * 2,
         out_specs=[hbm] * 2,
         scratch_shapes=[pltpu.SemaphoreType.DMA((2,))],
+        compiler_params=pltpu.CompilerParams(vmem_limit_bytes=1024 * 1024),
     )(*done)
 
 

time: 31 us -> 39.5 us (1.27); the launches traced: 30.9 us -> 38.9 us
  local copies, waits for them, and re-layouts: 1.5 us -> 10.8 us
  Pallas kernels: 28.7 us -> 27.4 us
    unnamed x4 -> x24, local copies, waits for them, and re-layouts: 1.5 us -> 10.8 us
    pallas_call x1, Pallas kernels: 2 us -> 0.89 us  [one_kernel(): pl.pallas_call(hand_over, out_shape=[jax.ShapeDtypeStruct(tl_pert.shape,...]
where the time goes in v5:
time: 39.5 us; the launch traced here: 38.9 us
  Pallas kernels  27.4 us (69%)
  local copies, waits for them, and re-layouts  10.8 us (27%)
  between operations  0.66 us (2%)
    pallas_call x1, Pallas kernels, one_kernel(): pl.pallas_call(functools.partial(step_kernel, half, bands, layout), out_s...  26.5 us
    unnamed x24, local copies, waits for them, and re-layouts  10.8 us
    pallas_call x1, Pallas kernels, one_kernel(): pl.pallas_call(hand_over, out_shape=[jax.ShapeDtypeStruct(tl_pert.shape,...  0.89 us

profile of v5, /device:TPU:0, one launch (start us, length us, event | category | flops | bytes accessed | tf_op | source)
XLA Modules:
  0.0 38.9 jit_solution(1291024713500882524)
XLA Ops:
  0.6 0.0 copy-start
  0.6 1.4 %copy-done = bf16[2,2,256,768]{3,2,1,0:T(8,128)(2,1)S(1)} copy-done((bf16[2,2,256,768]{3,2,1,0:T(8,128)(2,1)S(1)}, bf16[2,2,256,768]{3,2,1,0:T(8,128)(2,1)}, u32[]{:S(2)}) %copy-start) | copy-done | bytes 1572888
  2.0 0.0 copy-start.1
  2.0 1.4 %copy-done.1 = bf16[2,2,768,256]{3,2,1,0:T(8,128)(2,1)S(1)} copy-done((bf16[2,2,768,256]{3,2,1,0:T(8,128)(2,1)S(1)}, bf16[2,2,768,256]{3,2,1,0:T(8,128)(2,1)}, u32[]{:S(2)}) %copy-start.1) | copy-done | bytes 1572888
  3.5 0.0 copy-start.2
  3.5 1.0 %copy-done.2 = f32[8,4,2,1440]{3,2,1,0:T(2,128)S(1)} copy-done((f32[8,4,2,1440]{3,2,1,0:T(2,128)S(1)}, f32[8,4,2,1440]{3,2,1,0:T(2,128)}, u32[]{:S(2)}) %copy-start.2) | copy-done | bytes 368664
  4.5 0.0 copy-start.3
  4.5 1.0 %copy-done.3 = f32[8,4,2,1440]{3,2,1,0:T(2,128)S(1)} copy-done((f32[8,4,2,1440]{3,2,1,0:T(2,128)S(1)}, f32[8,4,2,1440]{3,2,1,0:T(2,128)}, u32[]{:S(2)}) %copy-start.3) | copy-done | bytes 368664
  5.4 0.0 copy-start.4
  5.4 0.8 %copy-done.4 = f32[4,2,1440]{2,1,0:T(2,128)S(1)} copy-done((f32[4,2,1440]{2,1,0:T(2,128)S(1)}, f32[4,2,1440]{2,1,0:T(2,128)}, u32[]{:S(2)}) %copy-start.4) | copy-done | bytes 46104
  6.2 0.0 copy-start.5
  6.2 0.8 %copy-done.5 = f32[4,2,1440]{2,1,0:T(2,128)S(1)} copy-done((f32[4,2,1440]{2,1,0:T(2,128)S(1)}, f32[4,2,1440]{2,1,0:T(2,128)}, u32[]{:S(2)}) %copy-start.5) | copy-done | bytes 46104
  7.0 0.0 copy-start.6
  7.0 0.8 %copy-done.6 = f32[4,2,1440]{2,1,0:T(2,128)S(1)} copy-done((f32[4,2,1440]{2,1,0:T(2,128)S(1)}, f32[4,2,1440]{2,1,0:T(2,128)}, u32[]{:S(2)}) %copy-start.6) | copy-done | bytes 46104
  7.8 0.0 copy-start.7
  7.8 0.8 %copy-done.7 = f32[8,2,720]{2,1,0:T(2,128)S(1)} copy-done((f32[8,2,720]{2,1,0:T(2,128)S(1)}, f32[8,2,720]{2,1,0:T(2,128)}, u32[]{:S(2)}) %copy-start.7) | copy-done | bytes 46104
  8.6 0.0 copy-start.8
  8.6 0.8 %copy-done.8 = f32[8,8,8]{2,1,0:T(8,128)S(1)} copy-done((f32[8,8,8]{2,1,0:T(8,128)S(1)}, f32[8,8,8]{2,1,0:T(8,128)}, u32[]{:S(2)}) %copy-start.8) | copy-done | bytes 2072
  9.4 0.0 copy-start.9
  9.4 0.8 %copy-done.9 = f32[8,8,8]{2,1,0:T(8,128)S(1)} copy-done((f32[8,8,8]{2,1,0:T(8,128)S(1)}, f32[8,8,8]{2,1,0:T(8,128)}, u32[]{:S(2)}) %copy-start.9) | copy-done | bytes 2072
  10.2 0.0 copy-start.10
  10.2 0.7 %copy-done.10 = s32[2]{0:T(128)S(1)} copy-done((s32[2]{0:T(128)S(1)}, s32[2]{0:T(128)}, u32[]{:S(2)}) %copy-start.10) | copy-done | bytes 32
  10.8 0.0 copy-start.11
  10.8 0.7 %copy-done.11 = s32[2,1]{0,1:T(1,128)S(1)} copy-done((s32[2,1]{0,1:T(1,128)S(1)}, s32[2,1]{0,1:T(1,128)}, u32[]{:S(2)}) %copy-start.11) | copy-done | bytes 32
  11.5 26.5 %shard_map.131 = (f32[8,4,2,1440]{3,2,1,0:T(2,128)S(1)}, f32[8,4,2,1440]{3,2,1,0:T(2,128)S(1)}) custom-call(s32[2]{0:T(128)S(1)} %copy-done.10, s32[2]{0:T(128)S(1)} %bitcast.1, f32[8,4,2,1440]{3,2,1,0:T(2,128)S(1)} %copy-done.2, f32[8,4,2,1440]{3,2,1,0:T(2,128)S(1)} %copy-done.3, f32[4,2,1440]{2,1,0:T(2,128)S(1)} %copy-done.4, f32[4,2,1440]{2,1,0:T(2,128)S(1)} %copy-done.5, ...), custom_call_target="tpu_custom_call" | custom-call | flops 1000000000 | bytes 8000000 | tf_op jit(solution)/shard_map/pallas_call | solution.py:656
  38.0 0.9 %shard_map.132 = (f32[8,4,2,1440]{3,2,1,0:T(2,128)}, f32[8,4,2,1440]{3,2,1,0:T(2,128)}) custom-call(f32[8,4,2,1440]{3,2,1,0:T(2,128)S(1)} %get-tuple-element.4.first, f32[8,4,2,1440]{3,2,1,0:T(2,128)S(1)} %get-tuple-element.5.second), custom_call_target="tpu_custom_call" | custom-call | tf_op jit(solution)/shard_map/pallas_call | solution.py:693
Async XLA Ops:
  0.6 1.4 %copy-start = (bf16[2,2,256,768]{3,2,1,0:T(8,128)(2,1)S(1)}, bf16[2,2,256,768]{3,2,1,0:T(8,128)(2,1)}, u32[]{:S(2)}) copy-start(bf16[2,2,256,768]{3,2,1,0:T(8,128)(2,1)} %constant.5.clone.bwd_hbm) | copy-start | bytes 4718596
  2.0 1.4 %copy-start.1 = (bf16[2,2,768,256]{3,2,1,0:T(8,128)(2,1)S(1)}, bf16[2,2,768,256]{3,2,1,0:T(8,128)(2,1)}, u32[]{:S(2)}) copy-start(bf16[2,2,768,256]{3,2,1,0:T(8,128)(2,1)} %constant.4.clone.fwd_hbm) | copy-start | bytes 4718596
  3.5 1.0 %copy-start.2 = (f32[8,4,2,1440]{3,2,1,0:T(2,128)S(1)}, f32[8,4,2,1440]{3,2,1,0:T(2,128)}, u32[]{:S(2)}) copy-start(f32[8,4,2,1440]{3,2,1,0:T(2,128)} %tl_hbm.1) | copy-start | bytes 1105924
  4.5 1.0 %copy-start.3 = (f32[8,4,2,1440]{3,2,1,0:T(2,128)S(1)}, f32[8,4,2,1440]{3,2,1,0:T(2,128)}, u32[]{:S(2)}) copy-start(f32[8,4,2,1440]{3,2,1,0:T(2,128)} %adj_hbm.1) | copy-start | bytes 1105924
  5.4 0.8 %copy-start.4 = (f32[4,2,1440]{2,1,0:T(2,128)S(1)}, f32[4,2,1440]{2,1,0:T(2,128)}, u32[]{:S(2)}) copy-start(f32[4,2,1440]{2,1,0:T(2,128)} %zonal_hbm.1) | copy-start | bytes 138244
  6.2 0.8 %copy-start.5 = (f32[4,2,1440]{2,1,0:T(2,128)S(1)}, f32[4,2,1440]{2,1,0:T(2,128)}, u32[]{:S(2)}) copy-start(f32[4,2,1440]{2,1,0:T(2,128)} %merid_hbm.1) | copy-start | bytes 138244
  7.0 0.8 %copy-start.6 = (f32[4,2,1440]{2,1,0:T(2,128)S(1)}, f32[4,2,1440]{2,1,0:T(2,128)}, u32[]{:S(2)}) copy-start(f32[4,2,1440]{2,1,0:T(2,128)} %vert_hbm.1) | copy-start | bytes 138244
  7.8 0.8 %copy-start.7 = (f32[8,2,720]{2,1,0:T(2,128)S(1)}, f32[8,2,720]{2,1,0:T(2,128)}, u32[]{:S(2)}) copy-start(f32[8,2,720]{2,1,0:T(2,128)} %state_hbm.1) | copy-start | bytes 138244
  8.6 0.8 %copy-start.8 = (f32[8,8,8]{2,1,0:T(8,128)S(1)}, f32[8,8,8]{2,1,0:T(8,128)}, u32[]{:S(2)}) copy-start(f32[8,8,8]{2,1,0:T(8,128)} %op_hbm.1) | copy-start | bytes 6148
  9.4 0.8 %copy-start.9 = (f32[8,8,8]{2,1,0:T(8,128)S(1)}, f32[8,8,8]{2,1,0:T(8,128)}, u32[]{:S(2)}) copy-start(f32[8,8,8]{2,1,0:T(8,128)} %remap_hbm.1) | copy-start | bytes 6148
  10.2 0.7 %copy-start.10 = (s32[2]{0:T(128)S(1)}, s32[2]{0:T(128)}, u32[]{:S(2)}) copy-start(s32[2]{0:T(128)} %cutoffs.1) | copy-start | bytes 28
  10.8 0.7 %copy-start.11 = (s32[2,1]{0,1:T(1,128)S(1)}, s32[2,1]{0,1:T(1,128)}, u32[]{:S(2)}) copy-start(s32[2,1]{0,1:T(1,128)} %param.21) | copy-start | bytes 28

commit v6 on v5

--- a/solution.py
+++ b/solution.py
@@ -434,52 +434,63 @@
         before = jnp.where(lane == 0, across[:, half - 1 : half], pltpu.roll(z, 1, 1))
         return after - before
 
+    spots = tiles // 2
+
     def product(base, transposed, vec):
         result = []
         for k in range(8):
-            terms = [
-                mats[base + (8 * l + k if transposed else 8 * k + l)] * vec[l] for l in range(8)
-            ]
-            while len(terms) > 1:
-                terms = [a + b for a, b in zip(terms[::2], terms[1::2])]
-            result.append(terms[0])
+            total = [None] * spots
+            for l in range(8):
+                weight = mats[base + (8 * l + k if transposed else 8 * k + l)]
+                for t in range(spots):
+                    term = weight * vec[l][t]
+                    total[t] = term if l == 0 else total[t] + term
+            result.append(total)
         return result
 
     def physics(src, dst, i, part, adjoint):
         steps = jnp.full((8, LANES), cost[i], jnp.int32)
-
-        def tile(t, carry):
-            cols = pl.ds(pl.multiple_of(t * LANES, LANES), LANES)
-            state = [
-                jnp.broadcast_to(
-                    winds[l // 2, 12 + 2 * (l % 2) + i : 13 + 2 * (l % 2) + i, cols], (8, LANES)
+        cols = [pl.ds((part * spots + t) * LANES, LANES) for t in range(spots)]
+
+        def scale(vec):
+            result = []
+            for l in range(8):
+                row = 12 + 2 * (l % 2) + i
+                result.append(
+                    [
+                        jnp.broadcast_to(winds[l // 2, row : row + 1, cols[t]], (8, LANES))
+                        * vec[l][t]
+                        for t in range(spots)
+                    ]
                 )
-                for l in range(8)
+            return result
+
+        def sub_step(s, vec):
+            new = scale(product(0, adjoint, vec))
+            active = s < steps
+            return [
+                [jnp.where(active, n, v) for n, v in zip(news, olds)]
+                for news, olds in zip(new, vec)
             ]
-            if adjoint:
-                vec = [src[l, i, :, cols] for l in range(8)]
-            else:
-                low = [src[0, l, i, :, cols] for l in range(5)]
-                high = [src[1, l, i, :, cols] for l in range(5)]
-                both = [low[3] + high[0], low[4] + high[1]]
-                vec = product(64, False, low[:3] + both + high[2:])
-
-            def sub_step(s, vec):
-                if adjoint:
-                    new = [d * v for d, v in zip(state, product(0, True, vec))]
+
+        if adjoint:
+            vec = [[src[l, i, :, at] for at in cols] for l in range(8)]
+            vec = scale(product(0, True, vec))
+        else:
+            vec = []
+            for l in range(8):
+                if l < 3:
+                    vec.append([src[0, l, i, :, at] for at in cols])
+                elif l > 4:
+                    vec.append([src[1, l - 3, i, :, at] for at in cols])
                 else:
-                    new = product(0, False, [d * v for d, v in zip(state, vec)])
-                active = s < steps
-                return [jnp.where(active, n, v) for n, v in zip(new, vec)]
-
-            vec = lax.fori_loop(0, SUBS, sub_step, vec)
-            if adjoint:
-                vec = product(64, True, vec)
-            for k in range(8):
-                dst[k, i, :, cols] = vec[k]
-            return carry
-
-        lax.fori_loop(part * tiles // 2, (part + 1) * tiles // 2, tile, 0)
+                    vec.append([src[0, l, i, :, at] + src[1, l - 3, i, :, at] for at in cols])
+            vec = scale(product(64, False, vec))
+        vec = lax.fori_loop(1, SUBS, sub_step, vec)
+        vec = product(64, True, vec) if adjoint else product(0, False, vec)
+        for k in range(8):
+            for t in range(spots):
+                dst[k, i, :, cols[t]] = vec[k][t]
 
     for i in range(2):
         adj_out_cols[i].wait_recv()
@@ -684,7 +695,7 @@
             pltpu.SemaphoreType.DMA((10,)),
         ],
         compiler_params=pltpu.CompilerParams(
-            collective_id=0, has_side_effects=True, vmem_limit_bytes=48 * 1024 * 1024
+            collective_id=0, has_side_effects=True, vmem_limit_bytes=56 * 1024 * 1024
         ),
         cost_estimate=pl.CostEstimate(
             flops=10**9, bytes_accessed=8 * 10**6, transcendentals=0

time: 39.5 us -> 28.2 us (0.71); the launches traced: 38.9 us -> 28.1 us
  local copies, waits for them, and re-layouts: 10.8 us -> 0 us
    unnamed x24 -> x0, local copies, waits for them, and re-layouts: 10.8 us -> none
where the time goes in v6:
time: 28.2 us; the launch traced here: 28.1 us
  Pallas kernels  27.4 us (97%)
  between operations  0.64 us (2%)
    pallas_call x1, Pallas kernels, one_kernel(): pl.pallas_call(functools.partial(step_kernel, half, bands, layout), out_s...  26.5 us
    pallas_call x1, Pallas kernels, one_kernel(): pl.pallas_call(hand_over, out_shape=[jax.ShapeDtypeStruct(tl_pert.shape,...  0.89 us

profile of v6, /device:TPU:0, one launch (start us, length us, event | category | flops | bytes accessed | tf_op | source)
XLA Modules:
  0.0 28.1 jit_solution(9355327859358232603)
XLA Ops:
  0.6 26.5 %shard_map.131 = (f32[8,4,2,1440]{3,2,1,0:T(2,128)S(1)}, f32[8,4,2,1440]{3,2,1,0:T(2,128)S(1)}) custom-call(s32[2]{0:T(128)} %cutoffs.1, s32[2]{0:T(128)} %bitcast.1, f32[8,4,2,1440]{3,2,1,0:T(2,128)} %tl_hbm.1, f32[8,4,2,1440]{3,2,1,0:T(2,128)} %adj_hbm.1, f32[4,2,1440]{2,1,0:T(2,128)} %zonal_hbm.1, f32[4,2,1440]{2,1,0:T(2,128)} %merid_hbm.1, ...), custom_call_target="tpu_custom_call" | custom-call | flops 1000000000 | bytes 8000000 | tf_op jit(solution)/shard_map/pallas_call | solution.py:667
  27.2 0.9 %shard_map.132 = (f32[8,4,2,1440]{3,2,1,0:T(2,128)}, f32[8,4,2,1440]{3,2,1,0:T(2,128)}) custom-call(f32[8,4,2,1440]{3,2,1,0:T(2,128)S(1)} %get-tuple-element.4.first, f32[8,4,2,1440]{3,2,1,0:T(2,128)S(1)} %get-tuple-element.5.second), custom_call_target="tpu_custom_call" | custom-call | tf_op jit(solution)/shard_map/pallas_call | solution.py:704

commit v7 on v6

--- a/solution.py
+++ b/solution.py
@@ -322,7 +322,10 @@
         for number, (i, cols) in enumerate(pieces)
     ]
     tl_out_cols = [
-        remote(8 + i, tbuf.at[other, :, i], tcols.at[lev, :, i], other, lat) for i in range(2)
+        remote(
+            17 + number, tbuf.at[other, :, i, :, cols], tcols.at[lev, :, i, :, cols], other, lat
+        )
+        for number, (i, cols) in enumerate(pieces)
     ]
     tl_in_bands = [
         remote(
@@ -558,6 +561,13 @@
     def _():
         merid_down.start()
 
+    for i in range(2):
+        for part in range(2):
+            tl_out_cols[2 * i + part].wait_recv()
+            physics(tcols, tback, i, part, False)
+            tl_in_bands[2 * i + part].start()
+    tband[lev] = tback[mine]
+
     def vert_parts(k, carry):
         for h in range(2):
             for i in range(2):
@@ -581,13 +591,6 @@
         return carry
 
     lax.fori_loop(0, 4, zonal_parts, 0)
-
-    for i in range(2):
-        tl_out_cols[i].wait_recv()
-        for part in range(2):
-            physics(tcols, tback, i, part, False)
-            tl_in_bands[2 * i + part].start()
-    tband[lev] = tback[mine]
 
     def join(pair):
         return jnp.concatenate([block[:, :half] for block in pair], axis=1)
@@ -690,8 +693,8 @@
             pltpu.VMEM((512, LANES), F32),
             pltpu.VMEM((128, 8, LANES), F32),
             pltpu.VMEM((2, 2, 8, MODES), F32),
-            pltpu.SemaphoreType.DMA((17,)),
-            pltpu.SemaphoreType.DMA((17,)),
+            pltpu.SemaphoreType.DMA((21,)),
+            pltpu.SemaphoreType.DMA((21,)),
             pltpu.SemaphoreType.DMA((10,)),
         ],
         compiler_params=pltpu.CompilerParams(

time: 28.2 us -> 28.1 us (level)
  no operation moved by 1% of the time
where the time goes in v7:
time: 28.1 us; the launch traced here: 27.9 us
  Pallas kernels  27.2 us (97%)
  between operations  0.64 us (2%)
    pallas_call x1, Pallas kernels, one_kernel(): pl.pallas_call(functools.partial(step_kernel, half, bands, layout), out_s...  26.3 us
    pallas_call x1, Pallas kernels, one_kernel(): pl.pallas_call(hand_over, out_shape=[jax.ShapeDtypeStruct(tl_pert.shape,...  0.89 us

profile of v7, /device:TPU:0, one launch (start us, length us, event | category | flops | bytes accessed | tf_op | source)
XLA Modules:
  0.0 27.9 jit_solution(5260041105297516189)
XLA Ops:
  0.6 26.3 %shard_map.131 = (f32[8,4,2,1440]{3,2,1,0:T(2,128)S(1)}, f32[8,4,2,1440]{3,2,1,0:T(2,128)S(1)}) custom-call(s32[2]{0:T(128)} %cutoffs.1, s32[2]{0:T(128)} %bitcast.1, f32[8,4,2,1440]{3,2,1,0:T(2,128)} %tl_hbm.1, f32[8,4,2,1440]{3,2,1,0:T(2,128)} %adj_hbm.1, f32[4,2,1440]{2,1,0:T(2,128)} %zonal_hbm.1, f32[4,2,1440]{2,1,0:T(2,128)} %merid_hbm.1, ...), custom_call_target="tpu_custom_call" | custom-call | flops 1000000000 | bytes 8000000 | tf_op jit(solution)/shard_map/pallas_call | solution.py:670
  27.0 0.9 %shard_map.132 = (f32[8,4,2,1440]{3,2,1,0:T(2,128)}, f32[8,4,2,1440]{3,2,1,0:T(2,128)}) custom-call(f32[8,4,2,1440]{3,2,1,0:T(2,128)S(1)} %get-tuple-element.4.first, f32[8,4,2,1440]{3,2,1,0:T(2,128)S(1)} %get-tuple-element.5.second), custom_call_target="tpu_custom_call" | custom-call | tf_op jit(solution)/shard_map/pallas_call | solution.py:707
